TPU v7x, 256 devices: a whole 4x4x8 slice. The times are simulated.
256 devices in a mesh: dp: 4 (over y), expert: 64 (over z, x, core).
Axes of the slice: x: 4, y: 4, z: 8, core: 2. Of those that a mesh axis runs over, the one named last changes fastest.
Arguments:
- tokens: bfloat16 [16384, 4096], P(('dp', 'expert')), may hold values from -6 to 6
- expert_ids: int32 [16384, 8], P(('dp', 'expert')), may hold values from 0 to 63, all different within a row; in each aligned block of 64 rows (0 to 63, 64 to 127, ...) at most 9 rows name the same one
- gate_values: float32 [16384, 8], P(('dp', 'expert')), may hold values from 0.05 to 0.5
- swap_mask: int32 [32], replicated, may hold values from 0 to 1, as said below
- gate_weight: bfloat16 [64, 4096, 1536], P('expert', None, 'dp'), may hold values from -0.09375 to 0.09375
- up_weight: bfloat16 [64, 4096, 1536], P('expert', None, 'dp'), may hold values from -0.09375 to 0.09375
- down_weight: bfloat16 [64, 1536, 4096], P('expert', 'dp'), may hold values from -0.15625 to 0.15625
Outputs:
- mixed: bfloat16 [16384, 4096], P(('dp', 'expert'))
Inputs may be any that keep to these rules, and one draw needn't show every extreme that they name: `expert_ids`: within each aligned block of 64 tokens (the tokens of one device) no slot is chosen more than 9 times, and some slot is chosen exactly 9 times in some block. A token's 8 slots differ. `swap_mask`: at least one pair exchanges and at least one pair does not.
All inputs are finite; a program needn't handle non-finite values.
Results may differ from a plain program's by a relative error of at most 0.015.
Values may be sent and summed in bfloat16 or wider, within the bound.
No kernel may reach another device: no remote copies, remote signals or barrier semaphores. Data moves between devices by JAX's collectives and lax.ppermute only.
A program may use at most 128 MiB of HBM per device.

v0:
```python
import jax
import jax.numpy as jnp
from jax import lax
from jax.sharding import PartitionSpec as P


def partner(block, axis, apart):
    count = lax.axis_size(axis)
    route = []
    for low in range(count):
        high = low | 1 << apart
        if high != low and high < count:
            route += [(low, high), (high, low)]
    return lax.ppermute(block, axis, route)


def local(tokens, expert_ids, gate_values, swap_mask, gate_weight, up_weight, down_weight):
    expert_count = lax.axis_size("expert")
    half_size = expert_count // 2
    tok_count = tokens.shape[0]
    top_count = expert_ids.shape[1]
    width = tokens.shape[1]
    capacity = min(tok_count, tok_count * top_count // expert_count + 1)
    slot_total = expert_count * capacity
    my_index = lax.axis_index("expert")
    slot_iota = jnp.arange(expert_count, dtype=jnp.int32)
    flipped = swap_mask[slot_iota % half_size]
    chosen = expert_ids.reshape(-1)
    one_hot = (chosen[:, None] == slot_iota[None, :]).astype(jnp.int32)
    slot_rank = jnp.sum((jnp.cumsum(one_hot, axis=0) - one_hot) * one_hot, axis=1)
    moved = partner((gate_weight, up_weight, down_weight), "expert", expert_count.bit_length() - 2)
    keep_own = flipped[my_index] == 0
    w_gate = jnp.where(keep_own, gate_weight, moved[0])[0]
    w_up = jnp.where(keep_own, up_weight, moved[1])[0]
    w_down = jnp.where(keep_own, down_weight, moved[2])[0]
    position = (chosen * capacity + slot_rank).reshape(tok_count, top_count)
    slot_index = jnp.arange(slot_total, dtype=jnp.int32)
    matches = position[None, :, :] == slot_index[:, None, None]
    select_matrix = jnp.any(matches, axis=2).astype(jnp.bfloat16)
    send_rows = jnp.dot(select_matrix, tokens, preferred_element_type=jnp.float32).astype(
        jnp.bfloat16
    )
    send_rows = send_rows.reshape(expert_count, capacity, width)
    arrived = lax.all_to_all(send_rows, "expert", split_axis=0, concat_axis=0, tiled=True).reshape(
        slot_total, width
    )
    gathered = lax.all_gather(arrived, "dp", axis=0, tiled=True)
    gate_act = jnp.dot(gathered, w_gate, preferred_element_type=jnp.float32)
    up_act = jnp.dot(gathered, w_up, preferred_element_type=jnp.float32)
    hidden = (jax.nn.silu(gate_act) * up_act).astype(jnp.bfloat16)
    summed = lax.psum_scatter(
        jnp.dot(hidden, w_down, preferred_element_type=jnp.float32).astype(jnp.bfloat16),
        "dp",
        scatter_dimension=0,
        tiled=True,
    )
    expert_out = summed.reshape(expert_count, capacity, width)
    returned = lax.all_to_all(
        expert_out, "expert", split_axis=0, concat_axis=0, tiled=True
    ).reshape(slot_total, width)
    weights_table = jnp.sum(jnp.where(matches, gate_values[None, :, :], 0.0), axis=2)
    combine_matrix = jnp.transpose(weights_table)
    combined = jnp.dot(
        combine_matrix,
        returned.astype(jnp.float32),
        precision=lax.Precision.HIGHEST,
        preferred_element_type=jnp.float32,
    )
    return combined.astype(jnp.bfloat16)


def solution(mesh):
    placed = (
        P(("dp", "expert"), None),
        P(("dp", "expert"), None),
        P(("dp", "expert"), None),
        P(),
        P("expert", None, "dp"),
        P("expert", None, "dp"),
        P("expert", "dp", None),
    )
    return jax.shard_map(
        local, mesh=mesh, in_specs=placed, out_specs=P(("dp", "expert"), None), check_vma=False
    )
```

profile of v0, /device:TPU:4, one launch (start us, length us, event | category | flops | bytes accessed | tf_op | source)
XLA Modules:
  0.0 1061.6 jit_solution(10880572508696991003)
XLA Ops:
  6.5 0.0 copy-start
  6.5 0.0 all-gather.2.cloned.1.call-start
  6.5 0.8 copy.22
  7.4 0.1 eq.50
  7.5 0.1 eq.46
  7.6 1.2 reduce-window.6
  8.8 0.2 slice_reduce_fusion
  9.0 0.1 fusion.21
  9.2 0.1 reduce_sum.21
  9.3 0.1 copy.25
  9.3 0.7 multiply_add_fusion
  10.0 0.1 copy.26
  10.1 0.5 fusion.18
  10.6 0.0 copy-done
  10.6 3.6 convolution_convert_fusion.1
  14.2 8.1 reshape.71
  22.3 198.2 %all_to_all.10 = bf16[64,9,4096]{2,1,0:T(8,128)(2,1)} all-to-all(bf16[64,9,4096]{2,1,0:T(8,128)(2,1)} %reshape.71), channel_id=1, replica_groups=mesh['dp'=4,'expert'=64] {'expert'}, dimensions={0} | all-to-all | bytes 9437184 | tf_op jit(solution)/shard_map/all_to_all | solution.py:44
  220.5 8.5 reshape.72
  229.0 0.0 copy-start.2
  229.0 0.0 all-gather.2.cloned.1.call-update
  229.0 0.0 reduce-scatter.2.cloned.1.call-start
  229.1 0.1 collective-permute-start
  229.2 5.9 collective-permute-start.1
  235.1 0.1 collective-permute-start.2
  235.2 0.0 copy-done.2
  235.2 0.8 gather_fusion
  236.0 0.6 dynamic_slice.3
  237.3 151.2 %collective-permute-done = bf16[1,4096,384]{2,1,0:T(8,128)(2,1)} collective-permute-done((bf16[1,4096,384]{2,1,0:T(8,128)(2,1)}, bf16[1,4096,384]{2,1,0:T(8,128)(2,1)}, u32[]{:S(2)}, u32[]{:S(2)}) %collective-permute-start) | collective-permute-done | bytes 3145760 | tf_op jit(solution)/shard_map/ppermute | solution.py:14
  388.5 12.1 %all-gather.2.cloned.1.call-done = bf16[2304,4096]{1,0:T(8,128)(2,1)} async-done(((bf16[576,4096]{1,0:T(8,128)(2,1)}), bf16[2304,4096]{1,0:T(8,128)(2,1)}) %all-gather.2.cloned.1.call-update) | async-done | bytes 18874384 | tf_op jit(solution)/shard_map/all_gather | solution.py:47
  400.6 15.9 %fusion.7 = f32[2304,384]{1,0:T(8,128)} fusion(bf16[2304,4096]{1,0:T(8,128)(2,1)} %all-gather.2.cloned.1.call-done, bf16[1,4096,384]{2,1,0:T(8,128)(2,1)} %param.11, bf16[1,4096,384]{2,1,0:T(8,128)(2,1)} %collective-permute-done, pred[]{:T(512)} %bitcast.2), kind=kOutput, calls=%fused_computation.8 | convolution fusion | flops 7249330176 | bytes 28704768 | tf_op jit(solution)/shard_map/dot_general | solution.py:48
  416.5 148.0 %collective-permute-done.1 = bf16[1,4096,384]{2,1,0:T(8,128)(2,1)} collective-permute-done((bf16[1,4096,384]{2,1,0:T(8,128)(2,1)}, bf16[1,4096,384]{2,1,0:T(8,128)(2,1)}, u32[]{:S(2)}, u32[]{:S(2)}) %collective-permute-start.1) | collective-permute-done | bytes 3145760 | tf_op jit(solution)/shard_map/ppermute | solution.py:14
  564.5 76.8 %collective-permute-done.2 = bf16[1,384,4096]{2,1,0:T(8,128)(2,1)} collective-permute-done((bf16[1,384,4096]{2,1,0:T(8,128)(2,1)}, bf16[1,384,4096]{2,1,0:T(8,128)(2,1)}, u32[]{:S(2)}, u32[]{:S(2)}) %collective-permute-start.2) | collective-permute-done | bytes 3145760 | tf_op jit(solution)/shard_map/ppermute | solution.py:14
  641.3 27.8 %convolution_convert_fusion = bf16[2304,4096]{1,0:T(8,128)(2,1)} fusion(f32[2304,384]{1,0:T(8,128)} %fusion.7, bf16[2304,4096]{1,0:T(8,128)(2,1)} %all-gather.2.cloned.1.call-done, bf16[1,384,4096]{2,1,0:T(8,128)(2,1)} %param.13, bf16[1,384,4096]{2,1,0:T(8,128)(2,1)} %collective-permute-done.2, bf16[1,4096,384]{2,1,0:T(8,128)(2,1)} %param.12, ...), kind=kOutput, calls=%fused_computation.1 | convolution fusion | flops 14513405952 | bytes 53870592 | tf_op jit(solution)/shard_map/dot_general | solution.py:52
  669.1 0.0 reduce-scatter.2.cloned.1.call-update
  669.1 165.8 %reduce-scatter.2.cloned.1.call-done = bf16[576,4096]{1,0:T(8,128)(2,1)} async-done(((bf16[2304,4096]{1,0:T(8,128)(2,1)}), bf16[576,4096]{1,0:T(8,128)(2,1)}) %reduce-scatter.2.cloned.1.call-update) | async-done | bytes 4718608 | tf_op jit(solution)/shard_map/reduce_scatter | solution.py:51
  834.9 8.2 reshape.73
  843.1 0.0 copy-start.3
  843.1 10.9 %all-to-all-start.1 = ((bf16[64,9,4096]{2,1,0:T(8,128)(2,1)}), bf16[64,9,4096]{2,1,0:T(8,128)(2,1)}, u32[]{:S(2)}, u32[]{:S(2)}) async-start(bf16[64,9,4096]{2,1,0:T(8,128)(2,1)} %reshape.73), calls=%async_computation.2 | async-start | bytes 16777216 | tf_op jit(solution)/shard_map/all_to_all | solution.py:58
  854.0 0.0 copy-done.3
  854.0 0.1 copy.27
  854.0 0.5 select_reduce_fusion
  854.5 185.8 %all-to-all-done.1 = bf16[64,9,4096]{2,1,0:T(8,128)(2,1)} async-done(((bf16[64,9,4096]{2,1,0:T(8,128)(2,1)}), bf16[64,9,4096]{2,1,0:T(8,128)(2,1)}, u32[]{:S(2)}, u32[]{:S(2)}) %all-to-all-start.1) | async-done | bytes 4718624 | tf_op jit(solution)/shard_map/all_to_all | solution.py:58
  1040.3 0.0 copy-start.1
  1040.3 8.5 reshape.74
  1048.8 5.9 convolution_convert_fusion.2
  1054.8 0.0 copy-done.1
  (5 shorter events, 0.1 us)
Async XLA Ops:
  6.5 4.1 copy-start
  6.5 394.0 %all-gather.2.cloned.1.call-start = ((), (), s32[]{:S(2)}) async-start(), calls=%async_computation.3 | async-start | bytes 23592960 | tf_op jit(solution)/shard_map/all_gather | solution.py:47
  229.0 6.2 copy-start.2
  229.0 605.9 %reduce-scatter.2.cloned.1.call-start = ((), (), s32[]{:S(2)}) async-start(), calls=%async_computation.4 | async-start | bytes 23592960 | tf_op jit(solution)/shard_map/reduce_scatter | solution.py:51
  229.1 159.4 %collective-permute-start = (bf16[1,4096,384]{2,1,0:T(8,128)(2,1)}, bf16[1,4096,384]{2,1,0:T(8,128)(2,1)}, u32[]{:S(2)}, u32[]{:S(2)}) collective-permute-start(bf16[1,4096,384]{2,1,0:T(8,128)(2,1)} %param.11), channel_id=1, source_target_pairs={{0,32},{32,0},{1,33},{33,1},{2,34},{34,2},{3,35},{35,3},{4,36},{36... | collective-permute-start | bytes 9437192 | tf_op jit(solution)/shard_map/ppermute | solution.py:14
  229.2 335.3 %collective-permute-start.1 = (bf16[1,4096,384]{2,1,0:T(8,128)(2,1)}, bf16[1,4096,384]{2,1,0:T(8,128)(2,1)}, u32[]{:S(2)}, u32[]{:S(2)}) collective-permute-start(bf16[1,4096,384]{2,1,0:T(8,128)(2,1)} %param.12), channel_id=1, source_target_pairs={{0,32},{32,0},{1,33},{33,1},{2,34},{34,2},{3,35},{35,3},{4,36},{36... | collective-permute-start | bytes 9437192 | tf_op jit(solution)/shard_map/ppermute | solution.py:14
  235.1 406.2 %collective-permute-start.2 = (bf16[1,384,4096]{2,1,0:T(8,128)(2,1)}, bf16[1,384,4096]{2,1,0:T(8,128)(2,1)}, u32[]{:S(2)}, u32[]{:S(2)}) collective-permute-start(bf16[1,384,4096]{2,1,0:T(8,128)(2,1)} %param.13), channel_id=1, source_target_pairs={{0,32},{32,0},{1,33},{33,1},{2,34},{34,2},{3,35},{35,3},{4,36},{36... | collective-permute-start | bytes 9437192 | tf_op jit(solution)/shard_map/ppermute | solution.py:14
  843.1 10.9 %copy-start.3 = (f32[64,8]{0,1:T(8,128)S(1)}, f32[64,8]{0,1:T(8,128)}, u32[]{:S(2)}) copy-start(f32[64,8]{0,1:T(8,128)} %param.9) | copy-start | bytes 6148
  843.1 197.3 %all-to-all-start.1 = ((bf16[64,9,4096]{2,1,0:T(8,128)(2,1)}), bf16[64,9,4096]{2,1,0:T(8,128)(2,1)}, u32[]{:S(2)}, u32[]{:S(2)}) async-start(bf16[64,9,4096]{2,1,0:T(8,128)(2,1)} %reshape.73), calls=%async_computation.2 | async-start | bytes 16777216 | tf_op jit(solution)/shard_map/all_to_all | solution.py:58
  1040.3 14.4 %copy-start.1 = (bf16[64,4096]{1,0:T(8,128)(2,1)S(1)}, bf16[64,4096]{1,0:T(8,128)(2,1)}, u32[]{:S(2)}) copy-start(bf16[64,4096]{1,0:T(8,128)(2,1)} %param.7) | copy-start | bytes 1572868
Sparse Core Ops, SparseCore 0:
  229.1 171.3 all-gather.1
  669.2 165.6 reduce-scatter.1
where the time goes:
time: 1060 us
  waiting for transfers between devices  740 us (70%)
  blocking collectives  198 us (19%)
  matrix products  53.3 us (5%)
  local copies, waits for them, and re-layouts  36.2 us (3%)
  starting transfers between devices  17 us (2%)
  between operations  14.2 us (1%)
    ppermute x3, waiting for transfers between devices, partner(): return lax.ppermute(block, axis, route)  376 us
    all_to_all x1, blocking collectives, local(): lax.all_to_all(send_rows, 'expert', split_axis=0, concat_axis=0, tiled=True)  198 us
    all_to_all x1, waiting for transfers between devices, local(): lax.all_to_all(expert_out, 'expert', split_axis=0, concat_axis=0, tiled=T...  186 us
    reduce_scatter x1, waiting for transfers between devices, local(): lax.psum_scatter(jnp.dot(hidden, w_down, preferred_element_type=jnp.float...  166 us
    dot_general x1, matrix products, local(): jnp.dot(hidden, w_down, preferred_element_type=jnp.float32)  27.8 us
  transfers between devices with their start and end apart: 6, of which 6 were waited for; matrix products, arithmetic and copies ran while one was open for 2% of the time, Pallas kernels for 0%

commit v1 on v0

v1 whole, which is shorter than its diff:
```python
import functools
import jax
import jax.numpy as jnp
from jax import lax
from jax.experimental import pallas as pl
from jax.experimental.pallas import tpu as pltpu
from jax.sharding import Mesh, PartitionSpec as P

Y, Z, X, C = "y", "z", "x", "c"
ALL = (Y, Z, X, C)
XC = (X, C)
N_Y, N_Z, N_XC = 4, 8, 8
EXTRA = 128
VMEM = 48 << 20


def shift(block, axis, by):
    count = lax.axis_size(axis)
    return lax.ppermute(block, axis, [(i, (i + by) % count) for i in range(count)])


def after(value, *others):
    return lax.optimization_barrier((value, *others))[0]


def codes_of(expert_ids, swap_mask, capacity):
    experts = N_Z * N_XC
    slots = jnp.arange(experts, dtype=jnp.int32)
    flipped = swap_mask[slots % (experts // 2)]
    holder = jnp.where(flipped == 1, slots ^ (experts // 2), slots)
    chosen = expert_ids.reshape(-1)
    one_hot = (chosen[:, None] == slots[None, :]).astype(jnp.int32)
    rank = jnp.sum((jnp.cumsum(one_hot, axis=0) - one_hot) * one_hot, axis=1)
    held_by = jnp.sum(one_hot * holder[None, :], axis=1)
    return held_by.reshape(expert_ids.shape), rank.reshape(expert_ids.shape)


def pairs_of(extra, top, capacity):
    values = extra.astype(jnp.float32)
    held_by = values[:, :top].astype(jnp.int32)
    rank = values[:, top : 2 * top].astype(jnp.int32)
    gates = values[:, 2 * top : 3 * top]
    source = jnp.arange(extra.shape[0], dtype=jnp.int32)[:, None] // (extra.shape[0] // N_Z)
    here = held_by // N_XC == lax.axis_index(Z)
    row = (held_by % N_XC * N_Z + source) * capacity + rank
    return jnp.where(here, row, -1), gates


def woven(parts, block):
    if len(parts) == 1:
        return parts[0]
    count = parts[0].shape[0] // block
    return jnp.concatenate([p[i * block : (i + 1) * block] for i in range(count) for p in parts], axis=0)


def unwoven(value, groups, block):
    if groups == 1:
        return [value]
    count = value.shape[0] // (block * groups)
    return [
        jnp.concatenate([value[(i * groups + g) * block : (i * groups + g + 1) * block] for i in range(count)], axis=0)
        for g in range(groups)
    ]


def pick_kernel(groups, per_token, per_row, rows_ref, tokens_ref, out_ref, matrix):
    @pl.when(pl.program_id(0) == 0)
    def _():
        for g in range(groups):
            slot = lax.broadcasted_iota(jnp.int32, matrix.shape[1:], 0)
            hit = jnp.zeros(matrix.shape[1:], jnp.float32)
            for k in range(rows_ref.shape[1]):
                hit = jnp.where(rows_ref[g, k : k + 1, :] == slot, 1.0, hit)
            matrix[g] = hit.astype(matrix.dtype)

    parts = unwoven(tokens_ref[...], groups, per_token)
    found = [dot(matrix[g], parts[g]) for g in range(groups)]
    out_ref[...] = woven(found, per_row).astype(out_ref.dtype)


def pick(rows_t, tokens, width, per_token, per_row, tile):
    groups, top, count = rows_t.shape
    total = N_XC * per_row
    return pl.pallas_call(
        functools.partial(pick_kernel, groups, per_token, per_row),
        grid=(width // tile,),
        in_specs=[
            pl.BlockSpec((groups, top, count), lambda j: (0, 0, 0)),
            pl.BlockSpec((groups * count, tile), lambda j: (0, j)),
        ],
        out_specs=pl.BlockSpec((groups * total, tile), lambda j: (0, j)),
        out_shape=jax.ShapeDtypeStruct((groups * total, width), jnp.bfloat16),
        scratch_shapes=[pltpu.VMEM((groups, total, count), jnp.bfloat16)],
        compiler_params=pltpu.CompilerParams(vmem_limit_bytes=VMEM),
        cost_estimate=pl.CostEstimate(
            flops=2 * groups * total * count * width, bytes_accessed=2 * groups * (total + count) * width, transcendentals=0
        ),
    )(rows_t, tokens)


def mix_kernel(groups, per_token, per_row, rows_ref, gates_ref, back_ref, out_ref, matrix):
    @pl.when(pl.program_id(0) == 0)
    def _():
        for g in range(groups):
            slot = lax.broadcasted_iota(jnp.int32, matrix.shape[1:], 1)
            total = jnp.zeros(matrix.shape[1:], jnp.float32)
            for k in range(rows_ref.shape[2]):
                total = jnp.where(rows_ref[g, :, k : k + 1] == slot, gates_ref[g, :, k : k + 1], total)
            matrix[g] = total.astype(matrix.dtype)

    back = back_ref[...]
    if groups > 1:
        parts = [p.astype(jnp.bfloat16) for p in unwoven(back.astype(jnp.float32), groups, per_row)]
    else:
        parts = [back]
    found = [dot(matrix[g], parts[g]) for g in range(groups)]
    out_ref[...] = woven(found, per_token).astype(out_ref.dtype)


def mix(rows, gates, back, per_token, per_row, tile):
    groups, count, top = rows.shape
    total = N_XC * per_row
    width = back.shape[1]
    return pl.pallas_call(
        functools.partial(mix_kernel, groups, per_token, per_row),
        grid=(width // tile,),
        in_specs=[
            pl.BlockSpec((groups, count, top), lambda j: (0, 0, 0)),
            pl.BlockSpec((groups, count, top), lambda j: (0, 0, 0)),
            pl.BlockSpec((groups * total, tile), lambda j: (0, j)),
        ],
        out_specs=pl.BlockSpec((groups * count, tile), lambda j: (0, j)),
        out_shape=jax.ShapeDtypeStruct((groups * count, width), jnp.bfloat16),
        scratch_shapes=[pltpu.VMEM((groups, count, total), jnp.bfloat16)],
        compiler_params=pltpu.CompilerParams(vmem_limit_bytes=VMEM),
        cost_estimate=pl.CostEstimate(
            flops=2 * groups * total * count * width, bytes_accessed=2 * groups * (total + count) * width, transcendentals=0
        ),
    )(rows, gates, back)


def down_kernel(has_add, hidden_ref, own_ref, low_ref, high_ref, *refs):
    weights = jnp.concatenate([own_ref[...], low_ref[...], high_ref[...]], axis=0)
    result = dot(hidden_ref[...], weights)
    if has_add:
        result = result + refs[0][...].astype(jnp.float32)
    refs[-1][...] = result.astype(refs[-1].dtype)


def down(hidden, own, low, high, first, width, tile, add=None):
    count, units = hidden.shape
    at = first // tile
    half = low.shape[0]
    extra = [] if add is None else [add]
    return pl.pallas_call(
        functools.partial(down_kernel, add is not None),
        grid=(width // tile,),
        in_specs=[
            pl.BlockSpec((count, units), lambda j: (0, 0)),
            pl.BlockSpec((own.shape[0], tile), lambda j: (0, j + at)),
            pl.BlockSpec((half, tile), lambda j: (0, j + at)),
            pl.BlockSpec((half, tile), lambda j: (0, j + at)),
        ]
        + [pl.BlockSpec((count, tile), lambda j: (0, j))] * len(extra),
        out_specs=pl.BlockSpec((count, tile), lambda j: (0, j)),
        out_shape=jax.ShapeDtypeStruct((count, width), jnp.bfloat16),
        compiler_params=pltpu.CompilerParams(vmem_limit_bytes=VMEM),
        cost_estimate=pl.CostEstimate(
            flops=2 * count * units * width, bytes_accessed=2 * (units + 2 * count) * width, transcendentals=0
        ),
    )(hidden, own, low, high, *extra)


def dot(a, b):
    return jnp.dot(a, b, preferred_element_type=jnp.float32)


def exchange(rows):
    parts = rows.reshape(N_XC, rows.shape[0] // N_XC, rows.shape[1])
    return lax.all_to_all(parts, XC, split_axis=0, concat_axis=0, tiled=True)


def local(tokens, expert_ids, gate_values, swap_mask, gate_weight, up_weight, down_weight):
    tok_count, width = tokens.shape
    top = expert_ids.shape[1]
    experts = N_Z * N_XC
    capacity = min(tok_count, tok_count * top // experts + 1)
    cut = width // 2
    tile = min(512, cut)
    w_gate, w_up, w_down = gate_weight[0], up_weight[0], down_weight[0]
    units = w_gate.shape[1]
    half = units // 2

    held_by, rank = codes_of(expert_ids, swap_mask, capacity)
    extra = jnp.concatenate(
        [held_by.astype(jnp.bfloat16), rank.astype(jnp.bfloat16), gate_values.astype(jnp.bfloat16)], axis=1
    )
    extra = jnp.pad(extra, ((0, 0), (0, EXTRA - extra.shape[1])))
    late_in = jnp.concatenate([tokens[:, cut:], extra], axis=1)
    early_in = jnp.concatenate([tokens[:, :cut], extra], axis=1)
    early_other = shift(early_in, Y, 2)

    low = jnp.concatenate([w_gate[:, :half], w_up[:, :half]], axis=1)
    high = jnp.concatenate([w_gate[:, half:], w_up[:, half:]], axis=1)
    low, high = after((low, high), early_in)
    low_in, high_in = shift(low, Y, -1), shift(high, Y, 1)
    down_parts = after((w_down[:half], w_down[half:]), low_in, high_in)
    down_low, down_high = shift(down_parts[0], Y, -1), shift(down_parts[1], Y, 1)

    late_all = lax.all_gather(late_in, Z, axis=0, tiled=True)
    early_pair = jnp.concatenate([early_in, early_other], axis=0)
    early_pair = after(early_pair, late_in)
    early_all = lax.all_gather(early_pair, Z, axis=0, tiled=True)

    per = N_Z * capacity
    total = N_XC * 2 * per
    late_width = width - cut
    late_pairs, late_gates = pairs_of(late_all[:, late_width:], top, capacity)
    late_rows = pick(late_pairs.T[None], late_all, late_width, tok_count, per, tile)
    late_own = exchange(late_rows)
    part = N_XC // 2
    late_other_0 = shift(late_own[:part], Y, 2)
    late_other_1 = shift(after(late_own[part:], late_other_0), Y, 2)
    late_other = jnp.concatenate([late_other_0, late_other_1], axis=0)

    by_group = early_all[:, cut:].reshape(N_Z, 2, tok_count, EXTRA)
    early_pairs, early_gates = zip(
        *(pairs_of(by_group[:, g].reshape(N_Z * tok_count, EXTRA), top, capacity) for g in range(2))
    )
    early_pairs, early_gates = jnp.stack(early_pairs), jnp.stack(early_gates)
    early_rows = pick(jnp.swapaxes(early_pairs, 1, 2), early_all, cut, tok_count, per, tile)
    early_rows = after(early_rows, late_own, late_other_0, low_in, high_in)
    early_got = exchange(early_rows).reshape(total, cut)
    late_got = jnp.stack([late_own, late_other], axis=1).reshape(total, late_width)

    w_own = jnp.concatenate([w_gate, w_up], axis=1)
    w_in = jnp.concatenate([low_in, high_in], axis=1)
    act_own = dot(late_got, w_own[cut:]) + dot(early_got, w_own[:cut])
    act_in = dot(late_got, w_in[cut:]) + dot(early_got, w_in[:cut])
    hidden = jnp.concatenate(
        [
            jax.nn.silu(act_own[:, :units]) * act_own[:, units:],
            jax.nn.silu(act_in[:, :half]) * act_in[:, half:units],
            jax.nn.silu(act_in[:, units : units + half]) * act_in[:, units + half :],
        ],
        axis=1,
    ).astype(jnp.bfloat16)
    by_group = hidden.reshape(N_XC, 2, per, 2 * units)
    hidden_own = by_group[:, 0].reshape(N_XC * per, 2 * units)
    hidden_other = by_group[:, 1].reshape(N_XC * per, 2 * units)
    late_for_other = down(hidden_other, w_down, down_low, down_high, cut, late_width, tile)
    late_from_other = shift(late_for_other, Y, 2)
    early_out = down(after(hidden, late_for_other), w_down, down_low, down_high, 0, cut, tile)
    early_back = after(exchange(early_out), late_from_other).reshape(total, cut)
    early_mixed = mix(early_pairs, early_gates, early_back, tok_count, per, tile)
    early_sum = lax.psum_scatter(early_mixed, Z, scatter_dimension=0, tiled=True)
    early_final = early_sum[:tok_count].astype(jnp.float32) + shift(early_sum[tok_count:], Y, 2).astype(jnp.float32)

    late_out = down(hidden_own, w_down, down_low, down_high, cut, late_width, tile, late_from_other)
    late_back = exchange(late_out).reshape(N_XC * per, late_width)
    late_mixed = mix(late_pairs[None], late_gates[None], late_back, tok_count, per, tile)
    late_final = lax.psum_scatter(late_mixed, Z, scatter_dimension=0, tiled=True)
    return jnp.concatenate([early_final.astype(jnp.bfloat16), late_final], axis=1)


def solution(mesh):
    fine = Mesh(mesh.devices.reshape(N_Y, N_Z, N_XC // 2, 2), ALL)
    experts = (Z, X, C)
    placed = (
        P(ALL, None),
        P(ALL, None),
        P(ALL, None),
        P(),
        P(experts, None, Y),
        P(experts, None, Y),
        P(experts, Y, None),
    )
    return jax.shard_map(local, mesh=fine, in_specs=placed, out_specs=P(ALL, None), check_vma=False)
```

time: 1060 us -> 515 us (0.49)
  waiting for transfers between devices: 740 us -> 330 us
  blocking collectives: 198 us -> 0 us
  Pallas kernels: 0 us -> 42.4 us
  matrix products: 53.3 us -> 24.3 us
  starting transfers between devices: 17 us -> 38.1 us
  other arithmetic: 3.03 us -> 21.1 us
    ppermute x3 -> x9, waiting for transfers between devices: 376 us -> 152 us  [shift(): lax.ppermute(block, axis, [(i, (i + by) % count) for i in range(count)])]
    all_to_all x1 -> x0, blocking collectives: 198 us -> none  [local(): lax.all_to_all(send_rows, 'expert', split_axis=0, concat_axis=0, tiled=True)]
    all_to_all x1 -> x4, waiting for transfers between devices: 186 us -> 52.3 us  [exchange(): return lax.all_to_all(parts, XC, split_axis=0, concat_axis=0, tiled=True)]
    reduce_scatter x1 -> x2, waiting for transfers between devices: 166 us -> 38.7 us  [the longest x1 31.6 us: local(): lax.psum_scatter(late_mixed, Z, scatter_dimension=0, tiled=True)]
    all_gather x1 -> x2, waiting for transfers between devices: 12.1 us -> 87 us  [the longest x1 56.7 us: local(): early_all = lax.all_gather(early_pair, Z, axis=0, tiled=True)]
    pallas_call x0 -> x7, Pallas kernels: none -> 42.4 us  [the longest x3 17.2 us: down(): pl.pallas_call(functools.partial(down_kernel, add is not None), grid=(wid...]
    reshape x4 -> x0, local copies, waits for them, and re-layouts: 33.3 us -> none  [the longest x1 8.53 us: local(): lax.all_to_all(send_rows, 'expert', split_axis=0, concat_axis=0, tiled=True)]
    dot_general x4, matrix products: 53.3 us -> 24.3 us  [dot(): return jnp.dot(a, b, preferred_element_type=jnp.float32)]
  transfers between devices with their start and end apart: 6 -> 17, of which waited for: 6 -> 13; matrix products, arithmetic and copies ran while one was open for 2% -> 11% of each run, Pallas kernels for 0% -> 3%
where the time goes in v1:
time: 515 us; the launch traced here: 507 us
  waiting for transfers between devices  330 us (64%)
  Pallas kernels  42.4 us (8%)
  starting transfers between devices  38.1 us (7%)
  local copies, waits for them, and re-layouts  36.8 us (7%)
  matrix products  24.3 us (5%)
  other arithmetic  21.1 us (4%)
  between operations  14 us (3%)
    ppermute x9, waiting for transfers between devices, shift(): lax.ppermute(block, axis, [(i, (i + by) % count) for i in range(count)])  152 us
    all_gather x1, waiting for transfers between devices, local(): early_all = lax.all_gather(early_pair, Z, axis=0, tiled=True)  56.7 us
    all_to_all x4, waiting for transfers between devices, exchange(): return lax.all_to_all(parts, XC, split_axis=0, concat_axis=0, tiled=True)  52.3 us
    reduce_scatter x1, waiting for transfers between devices, local(): lax.psum_scatter(late_mixed, Z, scatter_dimension=0, tiled=True)  31.6 us
    all_gather x1, waiting for transfers between devices, local(): late_all = lax.all_gather(late_in, Z, axis=0, tiled=True)  30.3 us
    dot_general x4, matrix products, dot(): return jnp.dot(a, b, preferred_element_type=jnp.float32)  24.3 us
    all_to_all x4, starting transfers between devices, exchange(): return lax.all_to_all(parts, XC, split_axis=0, concat_axis=0, tiled=True)  22.6 us
    pallas_call x3, Pallas kernels, down(): pl.pallas_call(functools.partial(down_kernel, add is not None), grid=(wid...  17.2 us
  transfers between devices with their start and end apart: 17, of which 13 were waited for; matrix products, arithmetic and copies ran while one was open for 11% of the time, Pallas kernels for 3%

profile of v1, /device:TPU:4, one launch (start us, length us, event | category | flops | bytes accessed | tf_op | source)
XLA Modules:
  0.0 506.6 jit_solution(7976661685161252307)
XLA Ops:
  6.5 0.9 copy.53
  9.3 1.2 reduce-window.6
  11.1 1.1 fusion.56
  13.2 3.3 collective-permute-start
  16.5 6.9 %collective-permute-done = bf16[64,2176]{1,0:T(8,128)(2,1)S(1)} collective-permute-done((bf16[64,2176]{1,0:T(8,128)(2,1)}, bf16[64,2176]{1,0:T(8,128)(2,1)S(1)}, u32[]{:S(2)}, u32[]{:S(2)}) %collective-permute-start) | collective-permute-done | bytes 278560 | tf_op jit(solution)/shard_map/ppermute | solution.py:19
  23.4 0.9 pad_maximum_fusion.7
  24.3 3.1 fusion.53
  27.4 30.3 %all-gather.5.cloned.1.call-done.tokens_ref = bf16[512,2176]{1,0:T(8,128)(2,1)} async-done(((bf16[64,2176]{1,0:T(8,128)(2,1)}), bf16[512,2176]{1,0:T(8,128)(2,1)}) %all-gather.5.cloned.1.call-update) | async-done | bytes 2228240 | tf_op jit(solution)/shard_map/all_gather | solution.py:210
  57.7 1.1 slice_convert_fusion.6
  58.8 56.7 %all-gather.3.cloned.1.call-done.tokens_ref = bf16[1024,2176]{1,0:T(8,128)(2,1)} async-done(((bf16[128,2176]{1,0:T(8,128)(2,1)}), bf16[1024,2176]{1,0:T(8,128)(2,1)}) %all-gather.3.cloned.1.call-update) | async-done | bytes 4456464 | tf_op jit(solution)/shard_map/all_gather | solution.py:213
  115.5 1.0 slice.167
  116.6 1.6 fusion.16
  118.3 4.0 shard_map.73
  122.3 4.8 all-to-all-start
  127.1 3.5 fusion.52
  130.6 5.0 pad_maximum_fusion.3
  135.6 2.7 collective-permute-start.3
  138.3 15.6 %all-to-all-done = bf16[8,72,2048]{2,1,0:T(8,128)(2,1)S(1)} async-done(((bf16[8,72,2048]{2,1,0:T(8,128)(2,1)}), bf16[8,72,2048]{2,1,0:T(8,128)(2,1)S(1)}, u32[]{:S(2)}, u32[]{:S(2)}) %all-to-all-start) | async-done | bytes 2359328 | tf_op jit(solution)/shard_map/all_to_all | solution.py:180
  153.9 1.7 fusion.54
  155.6 3.2 collective-permute-start.1
  158.8 1.8 pad_add_fusion
  160.8 2.3 copy-done.4
  163.1 6.3 %shard_map.74 = bf16[1152,2048]{1,0:T(8,128)(2,1)} custom-call(s32[2,8,512]{2,1,0:T(8,128)S(1)} %copy.61.rows_ref, bf16[1024,2176]{1,0:T(8,128)(2,1)S(1)} %copy-done.4), custom_call_target="tpu_custom_call" | custom-call | flops 2415919104 | bytes 8912896 | tf_op jit(solution)/shard_map/pallas_call | solution.py:84
  169.4 62.2 %collective-permute-done.3 = bf16[4096,384]{1,0:T(8,128)(2,1)} collective-permute-done((bf16[4096,384]{1,0:T(8,128)(2,1)}, bf16[4096,384]{1,0:T(8,128)(2,1)}, u32[]{:S(2)}, u32[]{:S(2)}) %collective-permute-start.3) | collective-permute-done | bytes 3145760 | tf_op jit(solution)/shard_map/ppermute | solution.py:19
  231.6 3.4 collective-permute-done.4
  235.0 5.1 %all-to-all-start.1 = ((bf16[8,144,2048]{2,1,0:T(8,128)(2,1)}), bf16[8,144,2048]{2,1,0:T(8,128)(2,1)}, u32[]{:S(2)}, u32[]{:S(2)}) async-start(bf16[8,144,2048]{2,1,0:T(8,128)(2,1)} %bitcast.90), calls=%async_computation.1 | async-start | bytes 9437184 | tf_op jit(solution)/shard_map/all_to_all | solution.py:180
  240.7 1.8 slice_bitcast_fusion
  243.4 1.2 collective-permute-start.6
  244.6 2.2 constant_dynamic-update-slice_fusion.1
  246.8 2.5 constant_dynamic-update-slice_fusion
  249.3 21.4 %collective-permute-done.2 = bf16[4,72,2048]{2,1,0:T(8,128)(2,1)S(1)} collective-permute-done((bf16[4,72,2048]{2,1,0:T(8,128)(2,1)}, bf16[4,72,2048]{2,1,0:T(8,128)(2,1)S(1)}, u32[]{:S(2)}, u32[]{:S(2)}) %collective-permute-start.2) | collective-permute-done | bytes 1179680 | tf_op jit(solution)/shard_map/ppermute | solution.py:19
  270.7 1.5 maximum_bitcast_fusion
  272.7 2.4 copy-done.19
  275.3 1.5 copy-done.17
  276.8 5.6 %fusion.1 = f32[1152,768]{1,0:T(8,128)} fusion(bf16[1152,2048]{1,0:T(8,128)(2,1)S(1)} %bitcast.102, bf16[4096,384]{1,0:T(8,128)(2,1)S(1)} %bitcast.97, bf16[4096,384]{1,0:T(8,128)(2,1)S(1)} %bitcast.94), kind=kOutput, calls=%fused_computation.7 | convolution fusion | flops 3630170112 | bytes 14548992 | tf_op jit(solution)/shard_map/dot_general | solution.py:175
  282.4 9.9 %all-to-all-done.1 = bf16[8,144,2048]{2,1,0:T(8,128)(2,1)} async-done(((bf16[8,144,2048]{2,1,0:T(8,128)(2,1)}), bf16[8,144,2048]{2,1,0:T(8,128)(2,1)}, u32[]{:S(2)}, u32[]{:S(2)}) %all-to-all-start.1) | async-done | bytes 4718624 | tf_op jit(solution)/shard_map/all_to_all | solution.py:180
  292.4 7.0 %fusion.3 = f32[1152,768]{1,0:T(8,128)S(1)} fusion(bf16[1152,2048]{1,0:T(8,128)(2,1)} %bitcast.22, bf16[4096,768]{1,0:T(8,128)(2,1)} %copy-done.25), kind=kOutput, calls=%fused_computation.8 | convolution fusion | flops 3623878656 | bytes 11403264 | tf_op jit(solution)/shard_map/dot_general | solution.py:175
  299.4 5.9 %convolution_add_fusion = f32[1152,768]{1,0:T(8,128)S(1)} fusion(f32[1152,768]{1,0:T(8,128)S(1)} %fusion.3, bf16[1152,2048]{1,0:T(8,128)(2,1)S(1)} %bitcast.103, bf16[4096,768]{1,0:T(8,128)(2,1)} %copy-done.25), kind=kOutput, calls=%fused_computation.4 | convolution fusion | flops 3624763392 | bytes 14942208 | tf_op jit(solution)/shard_map/dot_general | solution.py:175
  305.3 5.7 %convolution_add_fusion.1 = f32[1152,768]{1,0:T(8,128)S(1)} fusion(f32[1152,768]{1,0:T(8,128)S(1)} %copy-done.26, bf16[1152,2048]{1,0:T(8,128)(2,1)} %bitcast.22, bf16[4096,384]{1,0:T(8,128)(2,1)S(1)} %bitcast.95, bf16[4096,384]{1,0:T(8,128)(2,1)S(1)} %bitcast.98), kind=kOutput, calls=%fused_computation.5 | convolution fusion | flops 3631054848 | bytes 18087936 | tf_op jit(solution)/shard_map/dot_general | solution.py:175
  312.7 1.1 fusion.55
  314.2 5.1 %shard_map.75 = bf16[576,2048]{1,0:T(8,128)(2,1)} custom-call(bf16[576,768]{1,0:T(8,128)(2,1)S(1)} %bitcast.83, bf16[384,4096]{1,0:T(8,128)(2,1)} %bitcast.86, bf16[192,4096]{1,0:T(8,128)(2,1)S(1)} %collective-permute-done.5.low_ref, bf16[192,4096]{1,0:T(8,128)(2,1)S(1)} %collective-permute-done.6.high_ref), custom_call_target="tpu_custom_call" | custom-call | flops 1811939328 | bytes 7864320 | tf_op jit(solution)/shard_map/pallas_call | solution.py:155
  319.3 6.7 %shard_map.76 = bf16[1152,2048]{1,0:T(8,128)(2,1)} custom-call(bf16[1152,768]{1,0:T(8,128)(2,1)S(1)} %pad_maximum_fusion.5.hidden_ref, bf16[384,4096]{1,0:T(8,128)(2,1)} %bitcast.87, bf16[192,4096]{1,0:T(8,128)(2,1)S(1)} %collective-permute-done.5.low_ref, bf16[192,4096]{1,0:T(8,128)(2,1)S(1)} %collective-permute-done.6.high_ref), custom_call_target="tpu_custom_call" | custom-call | flops 3623878656 | bytes 12582912 | tf_op jit(solution)/shard_map/pallas_call | solution.py:155
  325.9 7.7 %all-to-all-start.2 = ((bf16[8,144,2048]{2,1,0:T(8,128)(2,1)}), bf16[8,144,2048]{2,1,0:T(8,128)(2,1)}, u32[]{:S(2)}, u32[]{:S(2)}) async-start(bf16[8,144,2048]{2,1,0:T(8,128)(2,1)} %bitcast.101), calls=%async_computation.2 | async-start | bytes 9437184 | tf_op jit(solution)/shard_map/all_to_all | solution.py:180
  334.2 1.1 slice_bitcast_fusion.3
  335.3 1.1 slice_bitcast_fusion.4
  336.4 0.8 pad_maximum_fusion.8.gates_ref
  337.2 51.5 %collective-permute-done.7.refs_0_ = bf16[576,2048]{1,0:T(8,128)(2,1)} collective-permute-done((bf16[576,2048]{1,0:T(8,128)(2,1)}, bf16[576,2048]{1,0:T(8,128)(2,1)}, u32[]{:S(2)}, u32[]{:S(2)}) %collective-permute-start.7) | collective-permute-done | bytes 2359328 | tf_op jit(solution)/shard_map/ppermute | solution.py:19
  388.8 1.0 copy-done.7
  389.8 1.0 copy-done.8
  390.8 10.1 %shard_map.77 = bf16[1024,2048]{1,0:T(8,128)(2,1)S(1)} custom-call(s32[2,512,8]{2,1,0:T(8,128)S(1)} %copy-done.7, f32[2,512,8]{2,1,0:T(8,128)S(1)} %copy-done.8, bf16[1152,2048]{1,0:T(8,128)(2,1)} %bitcast.31.back_ref), custom_call_target="tpu_custom_call" | custom-call | flops 2415919104 | bytes 8912896 | tf_op jit(solution)/shard_map/pallas_call | solution.py:124
  400.9 2.0 copy-done.2
  403.0 1.2 copy-done.5
  404.1 5.4 %shard_map.78 = bf16[576,2048]{1,0:T(8,128)(2,1)} custom-call(bf16[576,768]{1,0:T(8,128)(2,1)S(1)} %bitcast.82, bf16[384,4096]{1,0:T(8,128)(2,1)} %bitcast.88, bf16[192,4096]{1,0:T(8,128)(2,1)S(1)} %collective-permute-done.5.low_ref, bf16[192,4096]{1,0:T(8,128)(2,1)S(1)} %collective-permute-done.6.high_ref, bf16[576,2048]{1,0:T(8,128)(2,1)} %collective-permute-done.7.refs_0_), custom_call_target="tpu_custom_call" | custom-call | flops 1811939328 | bytes 7864320 | tf_op jit(solution)/shard_map/pallas_call | solution.py:155
  409.6 4.9 all-to-all-start.3
  414.7 26.7 %all-to-all-done.3 = bf16[8,72,2048]{2,1,0:T(8,128)(2,1)S(1)} async-done(((bf16[8,72,2048]{2,1,0:T(8,128)(2,1)}), bf16[8,72,2048]{2,1,0:T(8,128)(2,1)S(1)}, u32[]{:S(2)}, u32[]{:S(2)}) %all-to-all-start.3) | async-done | bytes 2359328 | tf_op jit(solution)/shard_map/all_to_all | solution.py:180
  441.4 4.8 shard_map.79
  446.2 1.3 copy-done.3
  447.5 7.1 %reduce-scatter.3.cloned.1.call-done = bf16[128,2048]{1,0:T(8,128)(2,1)} async-done(((bf16[1024,2048]{1,0:T(8,128)(2,1)}), bf16[128,2048]{1,0:T(8,128)(2,1)}) %reduce-scatter.3.cloned.1.call-update) | async-done | bytes 524304 | tf_op jit(solution)/shard_map/reduce_scatter | solution.py:256
  454.6 1.0 slice.197
  455.6 3.1 collective-permute-start.8
  458.7 6.6 %collective-permute-done.8 = bf16[64,2048]{1,0:T(8,128)(2,1)S(1)} collective-permute-done((bf16[64,2048]{1,0:T(8,128)(2,1)S(1)}, bf16[64,2048]{1,0:T(8,128)(2,1)S(1)}, u32[]{:S(2)}, u32[]{:S(2)}) %collective-permute-start.8) | collective-permute-done | bytes 262176 | tf_op jit(solution)/shard_map/ppermute | solution.py:19
  465.3 1.0 add_convert_fusion
  466.3 31.6 %reduce-scatter.5.cloned.1.call-done = bf16[64,2048]{1,0:T(8,128)(2,1)} async-done(((bf16[512,2048]{1,0:T(8,128)(2,1)}), bf16[64,2048]{1,0:T(8,128)(2,1)}) %reduce-scatter.5.cloned.1.call-update) | async-done | bytes 262160 | tf_op jit(solution)/shard_map/reduce_scatter | solution.py:262
  497.9 1.8 pad_maximum_fusion.9
  (92 shorter events, 8.6 us)
Async XLA Ops:
  6.5 1.9 copy-start
  6.5 17.8 %copy-start.14 = (bf16[1,4096,384]{2,1,0:T(8,128)(2,1)S(1)}, bf16[1,4096,384]{2,1,0:T(8,128)(2,1)}, u32[]{:S(2)}) copy-start(bf16[1,4096,384]{2,1,0:T(8,128)(2,1)} %param.12) | copy-start | bytes 9437188
  6.5 51.1 %all-gather.5.cloned.1.call-start = ((), (), s32[]{:S(2)}) async-start(), calls=%async_computation.7 | async-start | bytes 2506752 | tf_op jit(solution)/shard_map/all_gather | solution.py:210
  13.1 102.4 %all-gather.3.cloned.1.call-start = ((), (), s32[]{:S(2)}) async-start(), calls=%async_computation.6 | async-start | bytes 5013504 | tf_op jit(solution)/shard_map/all_gather | solution.py:213
  13.2 10.2 %collective-permute-start = (bf16[64,2176]{1,0:T(8,128)(2,1)}, bf16[64,2176]{1,0:T(8,128)(2,1)S(1)}, u32[]{:S(2)}, u32[]{:S(2)}) collective-permute-start(bf16[64,2176]{1,0:T(8,128)(2,1)} %get-tuple-element.43), channel_id=1, source_target_pairs={{0,128},{64,192},{128,0},{192,64},{1,129},{65,193},{129,1},{193,65... | collective-permute-start | bytes 835592 | tf_op jit(solution)/shard_map/ppermute | solution.py:19
  57.7 60.6 %copy-start.6 = (bf16[512,2176]{1,0:T(8,128)(2,1)S(1)}, bf16[512,2176]{1,0:T(8,128)(2,1)}, u32[]{:S(2)}) copy-start(bf16[512,2176]{1,0:T(8,128)(2,1)} %all-gather.5.cloned.1.call-done.tokens_ref) | copy-start | bytes 6684676
  58.8 59.4 %copy-start.23 = (f32[512,128]{1,0:T(8,128)}, f32[512,128]{1,0:T(8,128)S(1)}, u32[]{:S(2)}) copy-start(f32[512,128]{1,0:T(8,128)S(1)} %slice_convert_fusion.6) | copy-start | bytes 786436
  116.5 1.6 copy-start.21
  116.5 1.6 copy-start.22
  122.3 31.7 %all-to-all-start = ((bf16[8,72,2048]{2,1,0:T(8,128)(2,1)}), bf16[8,72,2048]{2,1,0:T(8,128)(2,1)S(1)}, u32[]{:S(2)}, u32[]{:S(2)}) async-start(bf16[8,72,2048]{2,1,0:T(8,128)(2,1)} %bitcast.13), calls=%async_computation | async-start | bytes 4718592 | tf_op jit(solution)/shard_map/all_to_all | solution.py:180
  127.1 3.5 copy-start.12
  127.1 3.5 copy-start.13
  135.6 96.0 %collective-permute-start.3 = (bf16[4096,384]{1,0:T(8,128)(2,1)}, bf16[4096,384]{1,0:T(8,128)(2,1)}, u32[]{:S(2)}, u32[]{:S(2)}) collective-permute-start(bf16[4096,384]{1,0:T(8,128)(2,1)} %get-tuple-element.16), channel_id=1, source_target_pairs={{0,192},{64,0},{128,64},{192,128},{1,193},{65,1},{129,65},{193,129... | collective-permute-start | bytes 9437192 | tf_op jit(solution)/shard_map/ppermute | solution.py:19
  138.3 96.7 %collective-permute-start.4 = (bf16[4096,384]{1,0:T(8,128)(2,1)}, bf16[4096,384]{1,0:T(8,128)(2,1)}, u32[]{:S(2)}, u32[]{:S(2)}) collective-permute-start(bf16[4096,384]{1,0:T(8,128)(2,1)} %get-tuple-element.17), channel_id=1, source_target_pairs={{0,64},{64,128},{128,192},{192,0},{1,65},{65,129},{129,193},{193,1... | collective-permute-start | bytes 9437192 | tf_op jit(solution)/shard_map/ppermute | solution.py:19
  153.9 6.7 %copy-start.10 = (bf16[8,72,2048]{2,1,0:T(8,128)(2,1)}, bf16[8,72,2048]{2,1,0:T(8,128)(2,1)S(1)}, u32[]{:S(2)}) copy-start(bf16[8,72,2048]{2,1,0:T(8,128)(2,1)S(1)} %all-to-all-done) | copy-start | bytes 7077892
  155.6 79.4 %collective-permute-start.1 = (bf16[4,72,2048]{2,1,0:T(8,128)(2,1)}, bf16[4,72,2048]{2,1,0:T(8,128)(2,1)}, u32[]{:S(2)}, u32[]{:S(2)}) collective-permute-start(bf16[4,72,2048]{2,1,0:T(8,128)(2,1)} %get-tuple-element.34), channel_id=1, source_target_pairs={{0,128},{64,192},{128,0},{192,64},{1,129},{65,193},{129,1},{193,65... | collective-permute-start | bytes 3538952 | tf_op jit(solution)/shard_map/ppermute | solution.py:19
  160.8 2.3 copy-start.4
  235.0 5.7 %copy-start.9 = (bf16[1,384,4096]{2,1,0:T(8,128)(2,1)S(1)}, bf16[1,384,4096]{2,1,0:T(8,128)(2,1)}, u32[]{:S(2)}) copy-start(bf16[1,384,4096]{2,1,0:T(8,128)(2,1)} %param.13) | copy-start | bytes 9437188
  235.0 57.4 %all-to-all-start.1 = ((bf16[8,144,2048]{2,1,0:T(8,128)(2,1)}), bf16[8,144,2048]{2,1,0:T(8,128)(2,1)}, u32[]{:S(2)}, u32[]{:S(2)}) async-start(bf16[8,144,2048]{2,1,0:T(8,128)(2,1)} %bitcast.90), calls=%async_computation.1 | async-start | bytes 9437184 | tf_op jit(solution)/shard_map/all_to_all | solution.py:180
  240.1 30.6 %collective-permute-start.2 = (bf16[4,72,2048]{2,1,0:T(8,128)(2,1)}, bf16[4,72,2048]{2,1,0:T(8,128)(2,1)S(1)}, u32[]{:S(2)}, u32[]{:S(2)}) collective-permute-start(bf16[4,72,2048]{2,1,0:T(8,128)(2,1)} %get-tuple-element.15), channel_id=1, source_target_pairs={{0,128},{64,192},{128,0},{192,64},{1,129},{65,193},{129,1},{193,65... | collective-permute-start | bytes 3538952 | tf_op jit(solution)/shard_map/ppermute | solution.py:19
  242.6 71.6 %collective-permute-start.5 = (bf16[192,4096]{1,0:T(8,128)(2,1)}, bf16[192,4096]{1,0:T(8,128)(2,1)S(1)}, u32[]{:S(2)}, u32[]{:S(2)}) collective-permute-start(bf16[192,4096]{1,0:T(8,128)(2,1)} %get-tuple-element.19), channel_id=1, source_target_pairs={{0,192},{64,0},{128,64},{192,128},{1,193},{65,1},{129,65},{193,129... | collective-permute-start | bytes 4718600 | tf_op jit(solution)/shard_map/ppermute | solution.py:19
  243.4 70.8 %collective-permute-start.6 = (bf16[192,4096]{1,0:T(8,128)(2,1)}, bf16[192,4096]{1,0:T(8,128)(2,1)S(1)}, u32[]{:S(2)}, u32[]{:S(2)}) collective-permute-start(bf16[192,4096]{1,0:T(8,128)(2,1)} %get-tuple-element.20), channel_id=1, source_target_pairs={{0,64},{64,128},{128,192},{192,0},{1,65},{65,129},{129,193},{193,1... | collective-permute-start | bytes 4718600 | tf_op jit(solution)/shard_map/ppermute | solution.py:19
  249.3 22.9 %copy-start.25 = (bf16[4096,768]{1,0:T(8,128)(2,1)}, bf16[4096,768]{1,0:T(8,128)(2,1)S(1)}, u32[]{:S(2)}) copy-start(bf16[4096,768]{1,0:T(8,128)(2,1)S(1)} %constant_dynamic-update-slice_fusion) | copy-start | bytes 18874372
  249.3 22.9 %copy-start.11 = (bf16[8,72,2048]{2,1,0:T(8,128)(2,1)S(1)}, bf16[8,72,2048]{2,1,0:T(8,128)(2,1)}, u32[]{:S(2)}) copy-start(bf16[8,72,2048]{2,1,0:T(8,128)(2,1)} %copy-done.10) | copy-start | bytes 7077892
  272.2 3.1 copy-start.15
  272.2 4.5 copy-start.17
  272.7 2.4 copy-start.19
  292.4 7.0 %copy-start.20 = (bf16[8,2,72,2048]{3,2,1,0:T(8,128)(2,1)S(1)}, bf16[8,2,72,2048]{3,2,1,0:T(8,128)(2,1)}, u32[]{:S(2)}) copy-start(bf16[8,2,72,2048]{3,2,1,0:T(8,128)(2,1)} %copy-done.19) | copy-start | bytes 14155780
  299.3 6.0 %copy-start.16 = (bf16[1,4096,384]{2,1,0:T(8,128)(2,1)S(1)}, bf16[1,4096,384]{2,1,0:T(8,128)(2,1)}, u32[]{:S(2)}) copy-start(bf16[1,4096,384]{2,1,0:T(8,128)(2,1)} %param.12) | copy-start | bytes 9437188
  299.3 6.0 %copy-start.18 = (bf16[1,4096,384]{2,1,0:T(8,128)(2,1)S(1)}, bf16[1,4096,384]{2,1,0:T(8,128)(2,1)}, u32[]{:S(2)}) copy-start(bf16[1,4096,384]{2,1,0:T(8,128)(2,1)} %param.11) | copy-start | bytes 9437188
  299.4 6.0 %copy-start.26 = (f32[1152,768]{1,0:T(8,128)S(1)}, f32[1152,768]{1,0:T(8,128)}, u32[]{:S(2)}) copy-start(f32[1152,768]{1,0:T(8,128)} %fusion.1) | copy-start | bytes 10616836
  325.9 62.8 %all-to-all-start.2 = ((bf16[8,144,2048]{2,1,0:T(8,128)(2,1)}), bf16[8,144,2048]{2,1,0:T(8,128)(2,1)}, u32[]{:S(2)}, u32[]{:S(2)}) async-start(bf16[8,144,2048]{2,1,0:T(8,128)(2,1)} %bitcast.101), calls=%async_computation.2 | async-start | bytes 9437184 | tf_op jit(solution)/shard_map/all_to_all | solution.py:180
  333.6 121.0 %reduce-scatter.3.cloned.1.call-start = ((), (), s32[]{:S(2)}) async-start(), calls=%async_computation.8 | async-start | bytes 4718592 | tf_op jit(solution)/shard_map/reduce_scatter | solution.py:256
  333.6 55.1 %collective-permute-start.7 = (bf16[576,2048]{1,0:T(8,128)(2,1)}, bf16[576,2048]{1,0:T(8,128)(2,1)}, u32[]{:S(2)}, u32[]{:S(2)}) collective-permute-start(bf16[576,2048]{1,0:T(8,128)(2,1)} %shard_map.75), channel_id=1, source_target_pairs={{0,128},{64,192},{128,0},{192,64},{1,129},{65,193},{129,1},{193,65... | collective-permute-start | bytes 7077896 | tf_op jit(solution)/shard_map/ppermute | solution.py:19
  388.8 1.0 copy-start.7
  389.8 1.0 copy-start.8
  400.9 2.0 copy-start.2
  403.0 1.2 copy-start.5
  409.6 4.9 copy-start.24
  409.6 31.8 %all-to-all-start.3 = ((bf16[8,72,2048]{2,1,0:T(8,128)(2,1)}), bf16[8,72,2048]{2,1,0:T(8,128)(2,1)S(1)}, u32[]{:S(2)}, u32[]{:S(2)}) async-start(bf16[8,72,2048]{2,1,0:T(8,128)(2,1)} %bitcast.91), calls=%async_computation.4 | async-start | bytes 4718592 | tf_op jit(solution)/shard_map/all_to_all | solution.py:180
  414.5 83.3 %reduce-scatter.5.cloned.1.call-start = ((), (), s32[]{:S(2)}) async-start(), calls=%async_computation.9 | async-start | bytes 2359296 | tf_op jit(solution)/shard_map/reduce_scatter | solution.py:262
  441.4 58.3 %copy-start.1 = (s32[32]{0:T(128)S(1)}, s32[32]{0:T(128)}, u32[]{:S(2)}) copy-start(s32[32]{0:T(128)} %param.10) | copy-start | bytes 388
  446.2 1.3 copy-start.3
  455.6 9.7 %collective-permute-start.8 = (bf16[64,2048]{1,0:T(8,128)(2,1)S(1)}, bf16[64,2048]{1,0:T(8,128)(2,1)S(1)}, u32[]{:S(2)}, u32[]{:S(2)}) collective-permute-start(bf16[64,2048]{1,0:T(8,128)(2,1)S(1)} %slice.197), channel_id=1, source_target_pairs={{0,128},{64,192},{128,0},{192,64},{1,129},{65,193},{129,1},{193,65... | collective-permute-start | bytes 786440 | tf_op jit(solution)/shard_map/ppermute | solution.py:19
Sparse Core Ops, SparseCore 0:
  13.2 44.3 all-gather.4
  59.5 55.9 all-gather.2
  403.1 51.4 reduce-scatter.2
  457.0 40.8 reduce-scatter.4

commit v2 on v0

v2 whole, which is shorter than its diff:
```python
import functools
import jax
import jax.numpy as jnp
from jax import lax
from jax.experimental import pallas as pl
from jax.experimental.pallas import tpu as pltpu
from jax.sharding import Mesh, PartitionSpec as P

Y, Z, X, C = "y", "z", "x", "c"
ALL = (Y, Z, X, C)
XC = (X, C)
N_Y, N_Z, N_XC = 4, 8, 8
EXTRA = 128
VMEM = 20 << 20
FREE = pl.CostEstimate(flops=0, bytes_accessed=0, transcendentals=0)


def shift(block, axis, by):
    count = lax.axis_size(axis)
    return lax.ppermute(block, axis, [(i, (i + by) % count) for i in range(count)])


def after(value, *others):
    return lax.optimization_barrier((value, *others))[0]


def codes_kernel(mask_ref, tokens_ref, own_ref, other_ref, out_ref):
    count, width = tokens_ref.shape
    top = own_ref.shape[0] // 2
    experts = N_Z * N_XC
    slot = lax.broadcasted_iota(jnp.int32, (count, experts), 1)
    own = lax.broadcasted_iota(jnp.int32, (1, experts), 1)
    mask = jnp.concatenate([mask_ref[...], mask_ref[...]], axis=1)
    holder = jnp.where(mask == 1, own ^ (experts // 2), own).astype(jnp.float32)
    row = lax.broadcasted_iota(jnp.int32, (count, count), 0)
    earlier = (lax.broadcasted_iota(jnp.int32, (count, count), 1) < row).astype(jnp.bfloat16)
    lane = lax.broadcasted_iota(jnp.int32, (count, EXTRA), 1)
    out = jnp.zeros((count, EXTRA), jnp.float32)
    for ref, first in ((own_ref, 0), (other_ref, EXTRA // 2)):
        pairs = ref[...].T
        ids = pairs[:, :top].astype(jnp.int32)
        hits = [(ids[:, k : k + 1] == slot).astype(jnp.float32) for k in range(top)]
        chosen = functools.reduce(lambda p, q: p + q, hits)
        before = dot(earlier, chosen.astype(jnp.bfloat16))
        for k in range(top):
            out = jnp.where(lane == first + k, jnp.sum(hits[k] * holder, axis=1, keepdims=True), out)
            out = jnp.where(lane == first + top + k, jnp.sum(hits[k] * before, axis=1, keepdims=True), out)
            out = jnp.where(lane == first + 2 * top + k, pairs[:, top + k : top + k + 1], out)
    out_ref[:, :width] = tokens_ref[...]
    out_ref[:, width:] = out.astype(out_ref.dtype)


def with_codes(mask, tokens, own, other):
    return pl.pallas_call(
        codes_kernel,
        out_shape=jax.ShapeDtypeStruct((tokens.shape[0], tokens.shape[1] + EXTRA), jnp.bfloat16),
        cost_estimate=FREE,
    )(mask[None], tokens, own, other)


def rows_of(held_by, rank, token, per_z, capacity, z):
    held_by = held_by.astype(jnp.int32)
    row = ((held_by & (N_XC - 1)) * N_Z + token // per_z) * capacity + rank.astype(jnp.int32)
    return jnp.where(held_by // N_XC == z, row, -1)


def picks_kernel(first, top, capacity, z_ref, extra_ref, out_ref):
    across = extra_ref[...].astype(jnp.float32).T[first : first + 2 * top]
    count = across.shape[1]
    token = lax.broadcasted_iota(jnp.int32, (top, count), 1)
    row = rows_of(across[:top], across[top:], token, count // N_Z, capacity, z_ref[0])
    slot = lax.broadcasted_iota(jnp.int32, out_ref.shape, 0)
    hit = jnp.zeros(out_ref.shape, jnp.float32)
    for k in range(top):
        hit = jnp.where(row[k : k + 1] == slot, 1.0, hit)
    out_ref[...] = hit.astype(out_ref.dtype)


def mixes_kernel(first, top, capacity, z_ref, extra_ref, out_ref):
    values = extra_ref[:, first : first + 3 * top].astype(jnp.float32)
    count = values.shape[0]
    token = lax.broadcasted_iota(jnp.int32, (count, top), 0)
    row = rows_of(values[:, :top], values[:, top : 2 * top], token, count // N_Z, capacity, z_ref[0])
    slot = lax.broadcasted_iota(jnp.int32, out_ref.shape, 1)
    total = jnp.zeros(out_ref.shape, jnp.float32)
    for k in range(top):
        total = jnp.where(row[:, k : k + 1] == slot, values[:, 2 * top + k : 2 * top + k + 1], total)
    out_ref[...] = total.astype(out_ref.dtype)


def matrix(kernel, gathered, first, top, capacity, shape):
    count, width = gathered.shape
    return pl.pallas_call(
        functools.partial(kernel, first, top, capacity),
        grid=(1,),
        in_specs=[
            pl.BlockSpec(memory_space=pltpu.SMEM),
            pl.BlockSpec((count, EXTRA), lambda j: (0, width // EXTRA - 1)),
        ],
        out_specs=pl.BlockSpec(shape, lambda j: (0, 0)),
        out_shape=jax.ShapeDtypeStruct(shape, jnp.bfloat16),
        compiler_params=pltpu.CompilerParams(vmem_limit_bytes=VMEM),
        cost_estimate=FREE,
    )(lax.axis_index(Z).astype(jnp.int32)[None], gathered)


def apply_kernel(matrix_ref, value_ref, out_ref):
    out_ref[...] = dot(matrix_ref[...], value_ref[...]).astype(out_ref.dtype)


def apply(matrix, value, first, width, tile):
    rows, inner = matrix.shape
    at = first // tile
    return pl.pallas_call(
        apply_kernel,
        grid=(width // tile,),
        in_specs=[pl.BlockSpec((rows, inner), lambda j: (0, 0)), pl.BlockSpec((inner, tile), lambda j: (0, j + at))],
        out_specs=pl.BlockSpec((rows, tile), lambda j: (0, j)),
        out_shape=jax.ShapeDtypeStruct((rows, width), jnp.bfloat16),
        compiler_params=pltpu.CompilerParams(vmem_limit_bytes=VMEM),
        cost_estimate=FREE,
    )(matrix, value)


def sides_kernel(bounds, gate_ref, up_ref, *out_refs):
    half = gate_ref.shape[1] // 2
    gate, up = gate_ref[...], up_ref[...]
    low = jnp.concatenate([gate[:, :half], up[:, :half]], axis=1)
    high = jnp.concatenate([gate[:, half:], up[:, half:]], axis=1)
    step = pl.program_id(0)
    for i, (first, last) in enumerate(zip(bounds, bounds[1:])):

        @pl.when((step >= first) & (step < last))
        def _():
            out_refs[2 * i][...] = low
            out_refs[2 * i + 1][...] = high


def sides(gate, up, bounds, tile):
    rows, units = gate.shape
    steps = [bound // tile for bound in bounds]

    def spec(first, last):
        return pl.BlockSpec((tile, units), lambda j: (jnp.clip(j - first, 0, last - first - 1), 0))

    ranges = [r for r in zip(bounds, bounds[1:]) for _ in range(2)]
    outs = pl.pallas_call(
        functools.partial(sides_kernel, steps),
        grid=(rows // tile,),
        in_specs=[pl.BlockSpec((tile, units), lambda j: (j, 0))] * 2,
        out_specs=[spec(first // tile, last // tile) for first, last in ranges],
        out_shape=[jax.ShapeDtypeStruct((last - first, units), gate.dtype) for first, last in ranges],
        compiler_params=pltpu.CompilerParams(vmem_limit_bytes=VMEM),
        cost_estimate=FREE,
    )(gate, up)
    return list(zip(outs[::2], outs[1::2]))


def down_kernel(has_add, hidden_ref, own_ref, low_ref, high_ref, *refs):
    weights = jnp.concatenate([own_ref[...], low_ref[...], high_ref[...]], axis=0)
    result = dot(hidden_ref[...], weights)
    if has_add:
        result = result + refs[0][...].astype(jnp.float32)
    refs[-1][...] = result.astype(refs[-1].dtype)


def down(hidden, own, low, high, first, width, tile, add=None):
    count, units = hidden.shape
    at = first // tile
    half = low.shape[0]
    extra = [] if add is None else [add]
    return pl.pallas_call(
        functools.partial(down_kernel, add is not None),
        grid=(width // tile,),
        in_specs=[
            pl.BlockSpec((count, units), lambda j: (0, 0)),
            pl.BlockSpec((own.shape[0], tile), lambda j: (0, j + at)),
            pl.BlockSpec((half, tile), lambda j: (0, j + at)),
            pl.BlockSpec((half, tile), lambda j: (0, j + at)),
        ]
        + [pl.BlockSpec((count, tile), lambda j: (0, j))] * len(extra),
        out_specs=pl.BlockSpec((count, tile), lambda j: (0, j)),
        out_shape=jax.ShapeDtypeStruct((count, width), jnp.bfloat16),
        compiler_params=pltpu.CompilerParams(vmem_limit_bytes=VMEM),
        cost_estimate=FREE,
    )(hidden, own, low, high, *extra)


def dot(a, b):
    return jnp.dot(a, b, preferred_element_type=jnp.float32)


def exchange(rows):
    parts = rows.reshape(N_XC, rows.shape[0] // N_XC, rows.shape[1])
    return lax.all_to_all(parts, XC, split_axis=0, concat_axis=0, tiled=True).reshape(rows.shape)


def local(tokens, expert_ids, gate_values, swap_mask, gate_weight, up_weight, down_weight):
    tok_count, width = tokens.shape
    top = expert_ids.shape[1]
    experts = N_Z * N_XC
    capacity = min(tok_count, tok_count * top // experts + 1)
    cut = width // 2
    tile = min(512, cut)
    w_gate, w_up, w_down = gate_weight[0], up_weight[0], down_weight[0]
    units = w_gate.shape[1]
    half = units // 2

    pairs = jnp.concatenate([expert_ids.T.astype(jnp.float32), gate_values.T], axis=0)
    own_tokens = with_codes(swap_mask, tokens, pairs, shift(pairs, Y, 2))
    other_tokens = shift(after(tokens[:, :cut], own_tokens), Y, 2)

    def swap(parts):
        return shift(parts[0], Y, -1), shift(parts[1], Y, 1)

    bounds = [0, width // 16 * 6, width // 16 * 11, width]
    side_2, side_1, side_0 = sides(after(w_gate, own_tokens), w_up, bounds, width // 16)
    down_low, down_high = swap(after((w_down[:half], w_down[half:]), pairs))
    side_0 = swap(after(side_0, down_low, down_high, other_tokens))
    side_1 = swap(after(side_1, *side_0))
    side_2 = swap(after(side_2, *side_1))

    own_all = lax.all_gather(own_tokens, Z, axis=0, tiled=True)
    other_all = lax.all_gather(after(other_tokens, own_tokens), Z, axis=0, tiled=True)
    own_all = after(own_all, down_low, down_high)

    late_width = width - cut
    rows, count = N_XC * N_Z * capacity, N_Z * tok_count
    second = EXTRA // 2
    pick_own = matrix(picks_kernel, own_all, 0, top, capacity, (rows, count))
    late_rows = apply(pick_own, own_all, cut, late_width, tile)
    own_rows = apply(after(pick_own, late_rows), own_all, 0, cut, tile)
    own_late = exchange(after(late_rows, own_rows, *side_0))
    own_early = exchange(after(own_rows, own_late, *side_1))
    mix_own = matrix(mixes_kernel, after(own_all, own_rows), 0, top, capacity, (count, rows))
    pick_other = matrix(picks_kernel, after(own_all, mix_own), second, top, capacity, (rows, count))
    other_rows = apply(pick_other, other_all, 0, cut, tile)
    other_early = exchange(after(other_rows, own_early, *side_2))
    mix_other = matrix(mixes_kernel, after(own_all, other_rows), second, top, capacity, (count, rows))
    other_late = shift(after(own_late, *side_2), Y, 2)

    w_own = jnp.concatenate([w_gate, w_up], axis=1)
    w_in = jnp.concatenate([jnp.concatenate(side, axis=1) for side in (side_2, side_1, side_0)], axis=0)

    def hidden_of(late, early):
        act_own = dot(late, w_own[cut:]) + dot(early, w_own[:cut])
        act_in = dot(late, w_in[cut:]) + dot(early, w_in[:cut])
        return jnp.concatenate(
            [
                jax.nn.silu(act_own[:, :units]) * act_own[:, units:],
                jax.nn.silu(act_in[:, :half]) * act_in[:, half:units],
                jax.nn.silu(act_in[:, units : units + half]) * act_in[:, units + half :],
            ],
            axis=1,
        ).astype(jnp.bfloat16)

    early_down = (w_down, down_low, down_high, 0, cut, tile)
    late_down = (w_down, down_low, down_high, cut, late_width, tile)
    hidden_own = hidden_of(own_late, own_early)
    own_out = down(hidden_own, *early_down)
    own_back = exchange(after(own_out, other_early))
    hidden_other = hidden_of(other_late, other_early)
    late_for_other = down(hidden_other, *late_down)
    late_from_other = shift(late_for_other, Y, 2)
    other_out = down(after(hidden_other, late_for_other), *early_down)

    own_mixed = apply(mix_own, after(own_back, other_out), 0, cut, tile)
    own_sum = lax.psum_scatter(own_mixed, Z, scatter_dimension=0, tiled=True)
    other_back = after(exchange(other_out), own_sum)
    other_mixed = apply(mix_other, other_back, 0, cut, tile)
    other_sum = lax.psum_scatter(after(other_mixed, late_from_other), Z, scatter_dimension=0, tiled=True)
    early_final = own_sum.astype(jnp.float32) + shift(other_sum, Y, 2).astype(jnp.float32)

    late_out = down(hidden_own, *late_down, late_from_other)
    late_back = exchange(after(late_out, other_mixed))
    late_final = lax.psum_scatter(apply(mix_own, late_back, 0, late_width, tile), Z, scatter_dimension=0, tiled=True)
    return jnp.concatenate([early_final.astype(jnp.bfloat16), late_final], axis=1)


def solution(mesh):
    fine = Mesh(mesh.devices.reshape(N_Y, N_Z, N_XC // 2, 2), ALL)
    experts = (Z, X, C)
    placed = (
        P(ALL, None),
        P(ALL, None),
        P(ALL, None),
        P(),
        P(experts, None, Y),
        P(experts, None, Y),
        P(experts, Y, None),
    )
    return jax.shard_map(local, mesh=fine, in_specs=placed, out_specs=P(ALL, None), check_vma=False)
```

time: 1060 us -> 405 us (0.38)
  waiting for transfers between devices: 740 us -> 157 us
  blocking collectives: 198 us -> 31.9 us
  Pallas kernels: 0 us -> 50.6 us
  starting transfers between devices: 17 us -> 61.6 us
  matrix products: 53.3 us -> 36.8 us
    ppermute x3 -> x13, waiting for transfers between devices: 376 us -> 79.7 us  [shift(): lax.ppermute(block, axis, [(i, (i + by) % count) for i in range(count)])]
    all_to_all x1, blocking collectives: 198 us -> 31.9 us  [exchange(): lax.all_to_all(parts, XC, split_axis=0, concat_axis=0, tiled=True)]
    all_to_all x1 -> x5, waiting for transfers between devices: 186 us -> 26.6 us  [exchange(): lax.all_to_all(parts, XC, split_axis=0, concat_axis=0, tiled=True)]
    reduce_scatter x1 -> x3, waiting for transfers between devices: 166 us -> 42.3 us  [the longest x1 33.9 us: local(): lax.psum_scatter(apply(mix_own, late_back, 0, late_width, tile), Z, scatt...]
    pallas_call x0 -> x16, Pallas kernels: none -> 50.6 us  [the longest x6 20.6 us: apply(): pl.pallas_call(apply_kernel, grid=(width // tile,), in_specs=[pl.BlockSpe...]
    unnamed x10 -> x89, local copies, waits for them, and re-layouts: 0.93 us -> 36.4 us
    reshape x4 -> x0, local copies, waits for them, and re-layouts: 33.3 us -> none  [the longest x1 8.53 us: local(): lax.all_to_all(send_rows, 'expert', split_axis=0, concat_axis=0, tiled=True)]
    all_to_all x1 -> x5, starting transfers between devices: 10.9 us -> 28.8 us  [exchange(): lax.all_to_all(parts, XC, split_axis=0, concat_axis=0, tiled=True)]
  transfers between devices with their start and end apart: 6 -> 23, of which waited for: 6 -> 15; matrix products, arithmetic and copies ran while one was open for 2% -> 12% of each run, Pallas kernels for 0% -> 11%
where the time goes in v2:
time: 405 us; the launch traced here: 400 us
  waiting for transfers between devices  157 us (39%)
  starting transfers between devices  61.6 us (15%)
  Pallas kernels  50.6 us (12%)
  local copies, waits for them, and re-layouts  43.8 us (11%)
  matrix products  36.8 us (9%)
  blocking collectives  31.9 us (8%)
  between operations  13.8 us (3%)
  other arithmetic  4.87 us (1%)
    ppermute x13, waiting for transfers between devices, shift(): lax.ppermute(block, axis, [(i, (i + by) % count) for i in range(count)])  79.7 us
    dot_general x8, matrix products, dot(): return jnp.dot(a, b, preferred_element_type=jnp.float32)  36.8 us
    unnamed x89, local copies, waits for them, and re-layouts  36.4 us
    reduce_scatter x1, waiting for transfers between devices, local(): lax.psum_scatter(apply(mix_own, late_back, 0, late_width, tile), Z, scatt...  33.9 us
    all_to_all x1, blocking collectives, exchange(): lax.all_to_all(parts, XC, split_axis=0, concat_axis=0, tiled=True)  31.9 us
    all_to_all x5, starting transfers between devices, exchange(): lax.all_to_all(parts, XC, split_axis=0, concat_axis=0, tiled=True)  28.8 us
    all_to_all x5, waiting for transfers between devices, exchange(): lax.all_to_all(parts, XC, split_axis=0, concat_axis=0, tiled=True)  26.6 us
    ppermute x13, starting transfers between devices, shift(): lax.ppermute(block, axis, [(i, (i + by) % count) for i in range(count)])  23.1 us
  transfers between devices with their start and end apart: 23, of which 15 were waited for; matrix products, arithmetic and copies ran while one was open for 12% of the time, Pallas kernels for 11%

profile of v2, /device:TPU:4, one launch (start us, length us, event | category | flops | bytes accessed | tf_op | source)
XLA Modules:
  0.0 400.2 jit_solution(14875995041009946792)
XLA Ops:
  7.9 3.2 collective-permute-start
  11.1 2.0 collective-permute-done.other_ref
  13.7 3.2 shard_map.73
  17.0 4.1 %slice_bitcast_fusion = (bf16[192,4096]{1,0:T(8,128)(2,1)}, bf16[192,4096]{1,0:T(8,128)(2,1)}) fusion(bf16[1,384,4096]{2,1,0:T(8,128)(2,1)} %param.13), kind=kLoop, calls=%fused_computation.8 | loop fusion | bytes 6291456 | tf_op jit(solution)/shard_map/slice | solution.py:218
  21.0 3.0 collective-permute-start.1
  25.0 2.3 collective-permute-start.3
  27.3 5.4 %shard_map.78 = (bf16[1536,384]{1,0:T(8,128)(2,1)}, bf16[1536,384]{1,0:T(8,128)(2,1)}, bf16[1280,384]{1,0:T(8,128)(2,1)S(1)}, bf16[1280,384]{1,0:T(8,128)(2,1)S(...) custom-call(bf16[4096,384]{1,0:T(8,128)(2,1)S(1)} %bitcast.42, bf16[4096,384]{1,0:T(8,128)(2,1)S(1)} %bitcast.49), custom_call_target="tpu_custom_call" | custom-call | tf_op jit(solution)/shard_map/pallas_call | solution.py:147
  36.7 28.2 %collective-permute-done.3 = bf16[64,2048]{1,0:T(8,128)(2,1)S(1)} collective-permute-done((bf16[64,2048]{1,0:T(8,128)(2,1)S(1)}, bf16[64,2048]{1,0:T(8,128)(2,1)S(1)}, u32[]{:S(2)}, u32[]{:S(2)}) %collective-permute-start.3) | collective-permute-done | bytes 262176 | tf_op jit(solution)/shard_map/ppermute | solution.py:20
  66.1 1.7 collective-permute-start.5
  67.8 8.2 %all-gather.3.cloned.1.call-done.extra_ref.value_ref = bf16[512,4224]{1,0:T(8,128)(2,1)} async-done(((bf16[64,4224]{1,0:T(8,128)(2,1)}), bf16[512,4224]{1,0:T(8,128)(2,1)}) %all-gather.3.cloned.1.call-update) | async-done | bytes 4325392 | tf_op jit(solution)/shard_map/all_gather | solution.py:223
  76.0 2.2 copy-done
  78.2 1.8 shard_map.74.matrix_ref
  80.5 2.3 shard_map.75
  82.8 1.4 copy-done.13
  84.2 3.4 shard_map.76
  87.6 4.9 %all-to-all-start = ((bf16[8,72,2048]{2,1,0:T(8,128)(2,1)}), bf16[8,72,2048]{2,1,0:T(8,128)(2,1)}, u32[]{:S(2)}, u32[]{:S(2)}) async-start(bf16[8,72,2048]{2,1,0:T(8,128)(2,1)} %bitcast.36), calls=%async_computation | async-start | bytes 4718592 | tf_op jit(solution)/shard_map/all_to_all | solution.py:195
  92.6 2.7 collective-permute-start.6
  95.2 21.3 %collective-permute-done.6 = bf16[1280,384]{1,0:T(8,128)(2,1)S(1)} collective-permute-done((bf16[1280,384]{1,0:T(8,128)(2,1)S(1)}, bf16[1280,384]{1,0:T(8,128)(2,1)S(1)}, u32[]{:S(2)}, u32[]{:S(2)}) %collective-permute-start.6) | collective-permute-done | bytes 983072 | tf_op jit(solution)/shard_map/ppermute | solution.py:20
  116.6 3.5 collective-permute-done.7
  120.1 6.9 %all-to-all-start.1 = ((bf16[8,72,2048]{2,1,0:T(8,128)(2,1)}), bf16[8,72,2048]{2,1,0:T(8,128)(2,1)}, u32[]{:S(2)}, u32[]{:S(2)}) async-start(bf16[8,72,2048]{2,1,0:T(8,128)(2,1)} %bitcast.10), calls=%async_computation.1 | async-start | bytes 4718592 | tf_op jit(solution)/shard_map/all_to_all | solution.py:195
  126.9 2.7 collective-permute-start.8
  131.0 2.4 constant_dynamic-update-slice_fusion
  133.3 2.2 copy-done.2
  135.6 2.3 shard_map.77.matrix_ref
  138.7 1.8 shard_map.80.matrix_ref
  142.6 1.6 copy-done.33
  144.2 3.3 shard_map.81
  147.5 8.0 %collective-permute-done.8 = bf16[1536,384]{1,0:T(8,128)(2,1)} collective-permute-done((bf16[1536,384]{1,0:T(8,128)(2,1)}, bf16[1536,384]{1,0:T(8,128)(2,1)}, u32[]{:S(2)}, u32[]{:S(2)}) %collective-permute-start.8) | collective-permute-done | bytes 1179680 | tf_op jit(solution)/shard_map/ppermute | solution.py:20
  155.5 3.6 collective-permute-done.9
  159.1 5.4 %fusion.17 = f32[576,768]{1,0:T(8,128)} fusion(bf16[576,2048]{1,0:T(8,128)(2,1)} %bitcast.9, bf16[4096,384]{1,0:T(8,128)(2,1)S(1)} %bitcast.43, bf16[4096,384]{1,0:T(8,128)(2,1)} %bitcast.46), kind=kOutput, calls=%fused_computation.43 | convolution fusion | flops 1818230784 | bytes 10420224 | tf_op jit(solution)/shard_map/dot_general | solution.py:190
  164.5 4.8 %all-to-all-start.2 = ((bf16[8,72,2048]{2,1,0:T(8,128)(2,1)}), bf16[8,72,2048]{2,1,0:T(8,128)(2,1)}, u32[]{:S(2)}, u32[]{:S(2)}) async-start(bf16[8,72,2048]{2,1,0:T(8,128)(2,1)} %bitcast.13), calls=%async_computation.2 | async-start | bytes 4718592 | tf_op jit(solution)/shard_map/all_to_all | solution.py:195
  169.3 4.6 %convolution_add_fusion.3 = f32[576,768]{1,0:T(8,128)S(1)} fusion(f32[576,768]{1,0:T(8,128)} %fusion.17, bf16[576,2048]{1,0:T(8,128)(2,1)} %bitcast.11, bf16[4096,384]{1,0:T(8,128)(2,1)} %bitcast.47, bf16[4096,384]{1,0:T(8,128)(2,1)S(1)} %bitcast.44), kind=kOutput, calls=%fused_computation.13 | convolution fusion | flops 1818673152 | bytes 12189696 | tf_op jit(solution)/shard_map/dot_general | solution.py:190
  174.2 4.6 %fusion.3 = f32[576,768]{1,0:T(8,128)S(1)} fusion(bf16[576,2048]{1,0:T(8,128)(2,1)} %bitcast.11, bf16[1280,768]{1,0:T(8,128)(2,1)} %constant_dynamic-update-slice_fusion, bf16[1536,384]{1,0:T(8,128)(2,1)} %collective-permute-done.9, bf16[1536,384]{1,0:T(8,128)(2,1)} %collective-permute-done.8), kind=kOutput, calls=%fused_computation.20 | convolution fusion | flops 1821376512 | bytes 8454144 | tf_op jit(solution)/shard_map/dot_general | solution.py:190
  178.8 4.7 %convolution_add_fusion.2 = f32[576,768]{1,0:T(8,128)S(1)} fusion(f32[576,768]{1,0:T(8,128)S(1)} %fusion.3, bf16[576,2048]{1,0:T(8,128)(2,1)} %bitcast.9, bf16[1280,768]{1,0:T(8,128)(2,1)} %constant_dynamic-update-slice_fusion, bf16[1280,384]{1,0:T(8,128)(2,1)} %collective-permute-done.5, bf16[1280,384]{1,0:T(8,128)(2,1)} %collective-permute-done.4), kind=kOutput, calls=%fused_computation.12 | convolution fusion | flops 1821818880 | bytes 9830400 | tf_op jit(solution)/shard_map/dot_general | solution.py:190
  185.8 2.9 shard_map.79
  188.8 1.5 copy-done.14
  191.2 5.1 %all-to-all-done.2 = bf16[8,72,2048]{2,1,0:T(8,128)(2,1)} async-done(((bf16[8,72,2048]{2,1,0:T(8,128)(2,1)}), bf16[8,72,2048]{2,1,0:T(8,128)(2,1)}, u32[]{:S(2)}, u32[]{:S(2)}) %all-to-all-start.2) | async-done | bytes 2359328 | tf_op jit(solution)/shard_map/all_to_all | solution.py:195
  196.3 7.4 %all-to-all-start.3 = ((bf16[8,72,2048]{2,1,0:T(8,128)(2,1)}), bf16[8,72,2048]{2,1,0:T(8,128)(2,1)}, u32[]{:S(2)}, u32[]{:S(2)}) async-start(bf16[8,72,2048]{2,1,0:T(8,128)(2,1)} %bitcast.38), calls=%async_computation.3 | async-start | bytes 4718592 | tf_op jit(solution)/shard_map/all_to_all | solution.py:195
  203.7 9.6 %reduce-scatter.4.cloned.1.call-start = ((), (), s32[]{:S(2)}) async-start(), calls=%async_computation.11 | async-start | bytes 2359296 | tf_op jit(solution)/shard_map/reduce_scatter | solution.py:268
  213.3 4.7 %fusion.9 = f32[576,768]{1,0:T(8,128)S(1)} fusion(bf16[576,2048]{1,0:T(8,128)(2,1)} %bitcast.14, bf16[4096,384]{1,0:T(8,128)(2,1)} %bitcast.48, bf16[4096,384]{1,0:T(8,128)(2,1)} %bitcast.41), kind=kOutput, calls=%fused_computation.32 | convolution fusion | flops 1818230784 | bytes 10420224 | tf_op jit(solution)/shard_map/dot_general | solution.py:190
  218.1 3.7 convolution_add_fusion.1
  222.0 4.6 %fusion.4 = f32[576,768]{1,0:T(8,128)S(1)} fusion(bf16[576,2048]{1,0:T(8,128)(2,1)} %bitcast.14, bf16[1280,768]{1,0:T(8,128)(2,1)} %constant_dynamic-update-slice_fusion, bf16[1536,384]{1,0:T(8,128)(2,1)} %collective-permute-done.9, bf16[1536,384]{1,0:T(8,128)(2,1)} %collective-permute-done.8), kind=kOutput, calls=%fused_computation.21 | convolution fusion | flops 1821376512 | bytes 8454144 | tf_op jit(solution)/shard_map/dot_general | solution.py:190
  226.6 4.6 %convolution_add_fusion = f32[576,768]{1,0:T(8,128)S(1)} fusion(f32[576,768]{1,0:T(8,128)S(1)} %fusion.4, bf16[576,2048]{1,0:T(8,128)(2,1)} %collective-permute-done.10, bf16[1280,768]{1,0:T(8,128)(2,1)} %constant_dynamic-update-slice_fusion, bf16[1280,384]{1,0:T(8,128)(2,1)} %collective-permute-done.5, bf16[1280,384]{1,0:T(8,128)(2,1)} %collective-permute-done.4), kind=kOutput, calls=%fused_computation.10 | convolution fusion | flops 1821818880 | bytes 9830400 | tf_op jit(solution)/shard_map/dot_general | solution.py:190
  233.1 2.9 shard_map.82
  237.4 2.9 shard_map.83
  240.3 1.4 copy-done.15
  242.8 4.0 shard_map.84
  248.1 3.6 collective-permute-start.11
  251.7 4.8 %all-to-all-start.4 = ((bf16[8,72,2048]{2,1,0:T(8,128)(2,1)}), bf16[8,72,2048]{2,1,0:T(8,128)(2,1)}, u32[]{:S(2)}, u32[]{:S(2)}) async-start(bf16[8,72,2048]{2,1,0:T(8,128)(2,1)} %bitcast.39), calls=%async_computation.5 | async-start | bytes 4718592 | tf_op jit(solution)/shard_map/all_to_all | solution.py:195
  256.6 2.2 copy-done.3
  258.8 2.3 shard_map.85.matrix_ref
  261.9 21.6 %all-to-all-done.4 = bf16[8,72,2048]{2,1,0:T(8,128)(2,1)} async-done(((bf16[8,72,2048]{2,1,0:T(8,128)(2,1)}), bf16[8,72,2048]{2,1,0:T(8,128)(2,1)}, u32[]{:S(2)}, u32[]{:S(2)}) %all-to-all-start.4) | async-done | bytes 2359328 | tf_op jit(solution)/shard_map/all_to_all | solution.py:195
  283.5 8.4 %reduce-scatter.4.cloned.1.call-done = bf16[64,2048]{1,0:T(8,128)(2,1)} async-done(((bf16[512,2048]{1,0:T(8,128)(2,1)}), bf16[64,2048]{1,0:T(8,128)(2,1)}) %reduce-scatter.4.cloned.1.call-update) | async-done | bytes 262160 | tf_op jit(solution)/shard_map/reduce_scatter | solution.py:268
  293.0 4.0 shard_map.86
  298.3 5.3 %collective-permute-done.11.refs_0_ = bf16[576,2048]{1,0:T(8,128)(2,1)} collective-permute-done((bf16[576,2048]{1,0:T(8,128)(2,1)}, bf16[576,2048]{1,0:T(8,128)(2,1)}, u32[]{:S(2)}, u32[]{:S(2)}) %collective-permute-start.11) | collective-permute-done | bytes 2359328 | tf_op jit(solution)/shard_map/ppermute | solution.py:20
  303.7 1.4 copy-done.8
  305.1 1.4 copy-done.12
  307.7 4.4 %shard_map.87 = bf16[576,2048]{1,0:T(8,128)(2,1)S(1)} custom-call(bf16[576,768]{1,0:T(8,128)(2,1)S(1)} %copy-done.19, bf16[384,4096]{1,0:T(8,128)(2,1)S(1)} %bitcast.35, bf16[192,4096]{1,0:T(8,128)(2,1)S(1)} %copy-done.8, bf16[192,4096]{1,0:T(8,128)(2,1)S(1)} %copy-done.12, bf16[576,2048]{1,0:T(8,128)(2,1)} %collective-permute-done.11.refs_0_), custom_call_target="tpu_custom_call" | custom-call | tf_op jit(solution)/shard_map/pallas_call | solution.py:172
  312.1 31.9 %all_to_all.30 = bf16[8,72,2048]{2,1,0:T(8,128)(2,1)S(1)} all-to-all(bf16[8,72,2048]{2,1,0:T(8,128)(2,1)S(1)} %bitcast.40), channel_id=1, replica_groups=mesh['y'=4,'z'=8,'x'=4,'c'=2] {'x','c'}, dimensions={0} | all-to-all | bytes 4718592 | tf_op jit(solution)/shard_map/all_to_all | solution.py:195
  344.0 3.6 shard_map.88
  347.7 3.3 collective-permute-start.12
  351.0 6.7 %collective-permute-done.12 = bf16[64,2048]{1,0:T(8,128)(2,1)S(1)} collective-permute-done((bf16[64,2048]{1,0:T(8,128)(2,1)}, bf16[64,2048]{1,0:T(8,128)(2,1)S(1)}, u32[]{:S(2)}, u32[]{:S(2)}) %collective-permute-start.12) | collective-permute-done | bytes 262176 | tf_op jit(solution)/shard_map/ppermute | solution.py:20
  357.8 33.9 %reduce-scatter.8.cloned.1.call-done = bf16[64,2048]{1,0:T(8,128)(2,1)} async-done(((bf16[512,2048]{1,0:T(8,128)(2,1)}), bf16[64,2048]{1,0:T(8,128)(2,1)}) %reduce-scatter.8.cloned.1.call-update) | async-done | bytes 262160 | tf_op jit(solution)/shard_map/reduce_scatter | solution.py:276
  391.7 1.8 pad_maximum_fusion.11
  (114 shorter events, 27.0 us)
Async XLA Ops:
  6.5 69.5 %all-gather.3.cloned.1.call-start = ((), (), s32[]{:S(2)}) async-start(), calls=%async_computation.9 | async-start | bytes 4866048 | tf_op jit(solution)/shard_map/all_gather | solution.py:223
  7.9 5.2 %copy-start.42 = (f32[16,64]{1,0:T(8,128)}, f32[16,64]{1,0:T(8,128)S(1)}, u32[]{:S(2)}) copy-start(f32[16,64]{1,0:T(8,128)S(1)} %pad_maximum_fusion.14.own_ref) | copy-start | bytes 12292
  7.9 5.2 %collective-permute-start = (f32[16,64]{1,0:T(8,128)S(1)}, f32[16,64]{1,0:T(8,128)S(1)}, u32[]{:S(2)}, u32[]{:S(2)}) collective-permute-start(f32[16,64]{1,0:T(8,128)S(1)} %pad_maximum_fusion.14.own_ref), channel_id=1, source_target_pairs={{0,128},{64,192},{128,0},{192,64},{1,129},{65,193},{129,1},{193,65... | collective-permute-start | bytes 12296 | tf_op jit(solution)/shard_map/ppermute | solution.py:20
  16.9 124.5 %all-gather.5.cloned.1.call-start = ((), (), s32[]{:S(2)}) async-start(), calls=%async_computation.10 | async-start | bytes 2359296 | tf_op jit(solution)/shard_map/all_gather | solution.py:224
  16.9 10.4 %copy-start.23 = (bf16[1,4096,384]{2,1,0:T(8,128)(2,1)S(1)}, bf16[1,4096,384]{2,1,0:T(8,128)(2,1)}, u32[]{:S(2)}) copy-start(bf16[1,4096,384]{2,1,0:T(8,128)(2,1)} %param.11) | copy-start | bytes 9437188
  16.9 10.4 %copy-start.26 = (bf16[1,4096,384]{2,1,0:T(8,128)(2,1)S(1)}, bf16[1,4096,384]{2,1,0:T(8,128)(2,1)}, u32[]{:S(2)}) copy-start(bf16[1,4096,384]{2,1,0:T(8,128)(2,1)} %param.12) | copy-start | bytes 9437188
  21.0 43.8 %collective-permute-start.1 = (bf16[192,4096]{1,0:T(8,128)(2,1)}, bf16[192,4096]{1,0:T(8,128)(2,1)S(1)}, u32[]{:S(2)}, u32[]{:S(2)}) collective-permute-start(bf16[192,4096]{1,0:T(8,128)(2,1)} %get-tuple-element.37), channel_id=1, source_target_pairs={{0,192},{64,0},{128,64},{192,128},{1,193},{65,1},{129,65},{193,129... | collective-permute-start | bytes 4718600 | tf_op jit(solution)/shard_map/ppermute | solution.py:20
  24.0 41.7 %collective-permute-start.2 = (bf16[192,4096]{1,0:T(8,128)(2,1)}, bf16[192,4096]{1,0:T(8,128)(2,1)S(1)}, u32[]{:S(2)}, u32[]{:S(2)}) collective-permute-start(bf16[192,4096]{1,0:T(8,128)(2,1)} %get-tuple-element.38), channel_id=1, source_target_pairs={{0,64},{64,128},{128,192},{192,0},{1,65},{65,129},{129,193},{193,1... | collective-permute-start | bytes 4718600 | tf_op jit(solution)/shard_map/ppermute | solution.py:20
  25.0 39.8 %collective-permute-start.3 = (bf16[64,2048]{1,0:T(8,128)(2,1)S(1)}, bf16[64,2048]{1,0:T(8,128)(2,1)S(1)}, u32[]{:S(2)}, u32[]{:S(2)}) collective-permute-start(bf16[64,2048]{1,0:T(8,128)(2,1)S(1)} %slice.73), channel_id=1, source_target_pairs={{0,128},{64,192},{128,0},{192,64},{1,129},{65,193},{129,1},{193,65... | collective-permute-start | bytes 786440 | tf_op jit(solution)/shard_map/ppermute | solution.py:20
  32.8 1.0 copy-start.34
  33.7 1.0 copy-start.36
  34.7 1.0 copy-start.38
  35.7 1.0 copy-start.39
  64.9 3.0 copy-start.41
  64.9 15.2 %copy-start.5 = (bf16[192,4096]{1,0:T(8,128)(2,1)}, bf16[192,4096]{1,0:T(8,128)(2,1)S(1)}, u32[]{:S(2)}) copy-start(bf16[192,4096]{1,0:T(8,128)(2,1)S(1)} %collective-permute-done.1.low_ref) | copy-start | bytes 4718596
  65.8 14.3 %copy-start.9 = (bf16[192,4096]{1,0:T(8,128)(2,1)}, bf16[192,4096]{1,0:T(8,128)(2,1)S(1)}, u32[]{:S(2)}) copy-start(bf16[192,4096]{1,0:T(8,128)(2,1)S(1)} %collective-permute-done.2.high_ref) | copy-start | bytes 4718596
  65.8 21.7 %collective-permute-start.4 = (bf16[1280,384]{1,0:T(8,128)(2,1)}, bf16[1280,384]{1,0:T(8,128)(2,1)}, u32[]{:S(2)}, u32[]{:S(2)}) collective-permute-start(bf16[1280,384]{1,0:T(8,128)(2,1)} %copy-done.39), channel_id=1, source_target_pairs={{0,192},{64,0},{128,64},{192,128},{1,193},{65,1},{129,65},{193,129... | collective-permute-start | bytes 2949128 | tf_op jit(solution)/shard_map/ppermute | solution.py:20
  66.1 21.5 %collective-permute-start.5 = (bf16[1280,384]{1,0:T(8,128)(2,1)}, bf16[1280,384]{1,0:T(8,128)(2,1)}, u32[]{:S(2)}, u32[]{:S(2)}) collective-permute-start(bf16[1280,384]{1,0:T(8,128)(2,1)} %copy-done.38), channel_id=1, source_target_pairs={{0,64},{64,128},{128,192},{192,0},{1,65},{65,129},{129,193},{193,1... | collective-permute-start | bytes 2949128 | tf_op jit(solution)/shard_map/ppermute | solution.py:20
  76.0 2.2 copy-start
  78.2 2.2 copy-start.1
  82.8 1.4 copy-start.13
  87.6 4.9 %copy-start.37 = (bf16[1280,384]{1,0:T(8,128)(2,1)S(1)}, bf16[1280,384]{1,0:T(8,128)(2,1)}, u32[]{:S(2)}) copy-start(bf16[1280,384]{1,0:T(8,128)(2,1)} %copy-done.36) | copy-start | bytes 2949124
  87.6 7.6 %copy-start.35 = (bf16[1280,384]{1,0:T(8,128)(2,1)S(1)}, bf16[1280,384]{1,0:T(8,128)(2,1)}, u32[]{:S(2)}) copy-start(bf16[1280,384]{1,0:T(8,128)(2,1)} %copy-done.34) | copy-start | bytes 2949124
  87.6 32.5 %all-to-all-start = ((bf16[8,72,2048]{2,1,0:T(8,128)(2,1)}), bf16[8,72,2048]{2,1,0:T(8,128)(2,1)}, u32[]{:S(2)}, u32[]{:S(2)}) async-start(bf16[8,72,2048]{2,1,0:T(8,128)(2,1)} %bitcast.36), calls=%async_computation | async-start | bytes 4718592 | tf_op jit(solution)/shard_map/all_to_all | solution.py:195
  92.6 24.0 %collective-permute-start.6 = (bf16[1280,384]{1,0:T(8,128)(2,1)S(1)}, bf16[1280,384]{1,0:T(8,128)(2,1)S(1)}, u32[]{:S(2)}, u32[]{:S(2)}) collective-permute-start(bf16[1280,384]{1,0:T(8,128)(2,1)S(1)} %copy-done.37), channel_id=1, source_target_pairs={{0,192},{64,0},{128,64},{192,128},{1,193},{65,1},{129,65},{193,129... | collective-permute-start | bytes 2949128 | tf_op jit(solution)/shard_map/ppermute | solution.py:20
  95.2 24.8 %collective-permute-start.7 = (bf16[1280,384]{1,0:T(8,128)(2,1)S(1)}, bf16[1280,384]{1,0:T(8,128)(2,1)}, u32[]{:S(2)}, u32[]{:S(2)}) collective-permute-start(bf16[1280,384]{1,0:T(8,128)(2,1)S(1)} %copy-done.35), channel_id=1, source_target_pairs={{0,64},{64,128},{128,192},{192,0},{1,65},{65,129},{129,193},{193,1... | collective-permute-start | bytes 2949128 | tf_op jit(solution)/shard_map/ppermute | solution.py:20
  120.1 44.4 %all-to-all-start.1 = ((bf16[8,72,2048]{2,1,0:T(8,128)(2,1)}), bf16[8,72,2048]{2,1,0:T(8,128)(2,1)}, u32[]{:S(2)}, u32[]{:S(2)}) async-start(bf16[8,72,2048]{2,1,0:T(8,128)(2,1)} %bitcast.10), calls=%async_computation.1 | async-start | bytes 4718592 | tf_op jit(solution)/shard_map/all_to_all | solution.py:195
  126.9 28.5 %collective-permute-start.8 = (bf16[1536,384]{1,0:T(8,128)(2,1)}, bf16[1536,384]{1,0:T(8,128)(2,1)}, u32[]{:S(2)}, u32[]{:S(2)}) collective-permute-start(bf16[1536,384]{1,0:T(8,128)(2,1)} %get-tuple-element.56), channel_id=1, source_target_pairs={{0,192},{64,0},{128,64},{192,128},{1,193},{65,1},{129,65},{193,129... | collective-permute-start | bytes 3538952 | tf_op jit(solution)/shard_map/ppermute | solution.py:20
  129.6 29.5 %collective-permute-start.9 = (bf16[1536,384]{1,0:T(8,128)(2,1)}, bf16[1536,384]{1,0:T(8,128)(2,1)}, u32[]{:S(2)}, u32[]{:S(2)}) collective-permute-start(bf16[1536,384]{1,0:T(8,128)(2,1)} %get-tuple-element.57), channel_id=1, source_target_pairs={{0,64},{64,128},{128,192},{192,0},{1,65},{65,129},{129,193},{193,1... | collective-permute-start | bytes 3538952 | tf_op jit(solution)/shard_map/ppermute | solution.py:20
  133.3 2.2 copy-start.2
  141.4 17.8 %copy-start.24 = (bf16[1,4096,384]{2,1,0:T(8,128)(2,1)S(1)}, bf16[1,4096,384]{2,1,0:T(8,128)(2,1)}, u32[]{:S(2)}) copy-start(bf16[1,4096,384]{2,1,0:T(8,128)(2,1)} %param.11) | copy-start | bytes 9437188
  141.4 1.2 copy-start.31
  142.6 1.6 copy-start.33
  159.1 58.9 %collective-permute-start.10 = (bf16[576,2048]{1,0:T(8,128)(2,1)}, bf16[576,2048]{1,0:T(8,128)(2,1)}, u32[]{:S(2)}, u32[]{:S(2)}) collective-permute-start(bf16[576,2048]{1,0:T(8,128)(2,1)} %bitcast.9), channel_id=1, source_target_pairs={{0,128},{64,192},{128,0},{192,64},{1,129},{65,193},{129,1},{193,65... | collective-permute-start | bytes 7077896 | tf_op jit(solution)/shard_map/ppermute | solution.py:20
  164.5 31.8 %all-to-all-start.2 = ((bf16[8,72,2048]{2,1,0:T(8,128)(2,1)}), bf16[8,72,2048]{2,1,0:T(8,128)(2,1)}, u32[]{:S(2)}, u32[]{:S(2)}) async-start(bf16[8,72,2048]{2,1,0:T(8,128)(2,1)} %bitcast.13), calls=%async_computation.2 | async-start | bytes 4718592 | tf_op jit(solution)/shard_map/all_to_all | solution.py:195
  178.8 5.3 %copy-start.10 = (bf16[192,4096]{1,0:T(8,128)(2,1)S(1)}, bf16[192,4096]{1,0:T(8,128)(2,1)}, u32[]{:S(2)}) copy-start(bf16[192,4096]{1,0:T(8,128)(2,1)} %copy-done.9) | copy-start | bytes 4718596
  183.5 1.9 copy-start.4
  183.5 2.3 copy-start.6
  188.7 1.5 copy-start.14
  190.2 1.0 copy-start.18
  196.3 45.4 %all-to-all-start.3 = ((bf16[8,72,2048]{2,1,0:T(8,128)(2,1)}), bf16[8,72,2048]{2,1,0:T(8,128)(2,1)}, u32[]{:S(2)}, u32[]{:S(2)}) async-start(bf16[8,72,2048]{2,1,0:T(8,128)(2,1)} %bitcast.38), calls=%async_computation.3 | async-start | bytes 4718592 | tf_op jit(solution)/shard_map/all_to_all | solution.py:195
  203.7 88.2 %reduce-scatter.4.cloned.1.call-start = ((), (), s32[]{:S(2)}) async-start(), calls=%async_computation.11 | async-start | bytes 2359296 | tf_op jit(solution)/shard_map/reduce_scatter | solution.py:268
  213.3 4.8 %copy-start.25 = (bf16[1,4096,384]{2,1,0:T(8,128)(2,1)S(1)}, bf16[1,4096,384]{2,1,0:T(8,128)(2,1)}, u32[]{:S(2)}) copy-start(bf16[1,4096,384]{2,1,0:T(8,128)(2,1)} %param.11) | copy-start | bytes 9437188
  213.3 4.8 %copy-start.27 = (bf16[1,4096,384]{2,1,0:T(8,128)(2,1)S(1)}, bf16[1,4096,384]{2,1,0:T(8,128)(2,1)}, u32[]{:S(2)}) copy-start(bf16[1,4096,384]{2,1,0:T(8,128)(2,1)} %param.12) | copy-start | bytes 9437188
  231.2 1.4 copy-start.7
  231.2 1.9 copy-start.11
  236.0 1.4 copy-start.32
  240.3 1.4 copy-start.15
  241.7 1.1 copy-start.21
  246.8 1.3 copy-start.17
  248.1 55.5 %collective-permute-start.11 = (bf16[576,2048]{1,0:T(8,128)(2,1)}, bf16[576,2048]{1,0:T(8,128)(2,1)}, u32[]{:S(2)}, u32[]{:S(2)}) collective-permute-start(bf16[576,2048]{1,0:T(8,128)(2,1)} %copy-done.32), channel_id=1, source_target_pairs={{0,128},{64,192},{128,0},{192,64},{1,129},{65,193},{129,1},{193,65... | collective-permute-start | bytes 7077896 | tf_op jit(solution)/shard_map/ppermute | solution.py:20
  251.7 31.8 %all-to-all-start.4 = ((bf16[8,72,2048]{2,1,0:T(8,128)(2,1)}), bf16[8,72,2048]{2,1,0:T(8,128)(2,1)}, u32[]{:S(2)}, u32[]{:S(2)}) async-start(bf16[8,72,2048]{2,1,0:T(8,128)(2,1)} %bitcast.39), calls=%async_computation.5 | async-start | bytes 4718592 | tf_op jit(solution)/shard_map/all_to_all | solution.py:195
  256.6 91.1 %reduce-scatter.6.cloned.1.call-start = ((), (), s32[]{:S(2)}) async-start(), calls=%async_computation.12 | async-start | bytes 2359296 | tf_op jit(solution)/shard_map/reduce_scatter | solution.py:271
  256.6 2.2 copy-start.3
  261.1 0.9 copy-start.28
  291.9 1.1 copy-start.29
  297.0 1.3 copy-start.16
  303.6 88.1 %reduce-scatter.8.cloned.1.call-start = ((), (), s32[]{:S(2)}) async-start(), calls=%async_computation.13 | async-start | bytes 2359296 | tf_op jit(solution)/shard_map/reduce_scatter | solution.py:276
  303.7 1.4 copy-start.8
  305.1 1.4 copy-start.12
  306.5 1.2 copy-start.19
  312.1 31.9 %copy-start.22 = (bf16[512,576]{1,0:T(8,128)(2,1)S(1)}, bf16[512,576]{1,0:T(8,128)(2,1)}, u32[]{:S(2)}) copy-start(bf16[512,576]{1,0:T(8,128)(2,1)} %copy-done.20) | copy-start | bytes 1769476
  344.0 13.7 %copy-start.40 = (bf16[64,2048]{1,0:T(8,128)(2,1)S(1)}, bf16[64,2048]{1,0:T(8,128)(2,1)}, u32[]{:S(2)}) copy-start(bf16[64,2048]{1,0:T(8,128)(2,1)} %reduce-scatter.4.cloned.1.call-done) | copy-start | bytes 786436
  347.7 10.0 %collective-permute-start.12 = (bf16[64,2048]{1,0:T(8,128)(2,1)}, bf16[64,2048]{1,0:T(8,128)(2,1)S(1)}, u32[]{:S(2)}, u32[]{:S(2)}) collective-permute-start(bf16[64,2048]{1,0:T(8,128)(2,1)} %reduce-scatter.6.cloned.1.call-done), channel_id=1, source_target_pairs={{0,128},{64,192},{128,0},{192,64},{1,129},{65,193},{129,1},{193,65... | collective-permute-start | bytes 786440 | tf_op jit(solution)/shard_map/ppermute | solution.py:20
  (3 other events, 2.2 us)
Sparse Core Ops, SparseCore 0:
  17.0 58.9 all-gather.2
  77.8 39.6 all-gather.4
  248.3 43.6 reduce-scatter.3
  303.8 43.1 reduce-scatter.5
  349.4 42.2 reduce-scatter.7
